TPU v7x, 256 devices: a whole 4x4x8 slice. The times are simulated.
256 devices in a mesh: snode: 16 (over z, core), rhs: 16 (over x, y).
Axes of the slice: x: 4, y: 4, z: 8, core: 2. Of those that a mesh axis runs over, the one named last changes fastest.
Arguments:
- leaf_inv: bfloat16 [64, 512, 512], P('snode', 'rhs'), as said below
- leaf_panel: bfloat16 [64, 1024, 512], P('snode', 'rhs'), may hold values from -0.0625 to 0.0625
- leaf_rows: int32 [64, 1024], P('snode'), may hold values from 0 to 4095, as said below
- leaf_loads: bfloat16 [64, 512, 4096], P('snode', None, 'rhs'), may hold values from -6 to 6
- top_inv: bfloat16 [4096, 4096], P('snode', 'rhs'), as said below
- top_loads: bfloat16 [4096, 4096], P('snode', 'rhs'), may hold values from -6 to 6
Outputs:
- leaf_solution: float32 [64, 512, 4096], P('snode', None, 'rhs')
- top_solution: float32 [4096, 4096], P('snode', 'rhs')
Inputs may be any that keep to these rules, and one draw needn't show every extreme that they name: `leaf_rows`: the indices of one leaf are distinct; each aligned group of 4 consecutive leaves names every separator row exactly once. `leaf_inv`: lower triangular, diagonal between 0.6 and 1.4. `top_inv`: lower triangular, diagonal between 0.6 and 1.4.
All inputs are finite; a program needn't handle non-finite values.
Results may differ from a plain program's by a relative error of at most 0.0045.
Values may be sent and summed in bfloat16 or wider, within the bound.
No kernel may reach another device: no remote copies, remote signals or barrier semaphores. Data moves between devices by JAX's collectives and lax.ppermute only.
A program may use at most 64 MiB of HBM per device.

v0:
```python
import jax
import jax.numpy as jnp
from jax import lax
from jax.experimental import pallas as pl
from jax.experimental.pallas import tpu as pltpu
from jax.sharding import PartitionSpec as P

BF = jnp.bfloat16
F32 = jnp.float32
OFFSETS = (0, 3, 1, 2)
Z_OFFSETS = (0, 7, 1, 6, 2, 5, 3, 4)
ZS, XS, YS, CORES = 8, 4, 4, 2
VMEM = pl.BlockSpec(memory_space=pltpu.VMEM)
ANY = pl.BlockSpec(memory_space=pl.ANY)
SMEM = pl.BlockSpec(memory_space=pltpu.SMEM)
PARAMS = pltpu.CompilerParams(vmem_limit_bytes=50 * 1024 * 1024)


def move_rhs(a, dx, dy):
    pairs = [(4 * x + y, 4 * ((x + dx) % 4) + (y + dy) % 4) for x in range(XS) for y in range(YS)]
    return lax.ppermute(a, "rhs", pairs)


def move_z(a, d):
    return lax.ppermute(a, "snode", [(i, (i + 2 * d) % 16) for i in range(16)])


def swap_core(a):
    return lax.ppermute(a, "snode", [(i, i ^ 1) for i in range(16)])


def around(a, move):
    return move(a, 1), move(a, -1)


def far(before, after, move):
    half = before.shape[0] // 2
    return move(before[:half], 1), move(after[half:], -1)


def along_x(a, d):
    return move_rhs(a, d, 0)


def along_y(a, d):
    return move_rhs(a, 0, d)


def gather_factors(first, second, top_inv):
    across = lax.ppermute(top_inv, ("snode", "rhs"), [(16 * a + b, 16 * b + a) for a in range(16) for b in range(16)])
    a1, b1 = around(first, along_y), around(second, along_x)
    z1 = around(top_inv, move_z)
    a1, b1, z1, across = lax.optimization_barrier((a1, b1, z1, across))
    left = lax.all_gather(across, "rhs", axis=0, tiled=True)
    near_a = jnp.concatenate([first, *a1, *far(*a1, along_y)], axis=0)
    near_b = jnp.concatenate([second, *b1, *far(*b1, along_x)], axis=0)
    a2, b2 = around(near_a, along_x), around(near_b, along_y)
    z2 = move_z(z1[0], 1), move_z(z1[1], -1)
    z3 = move_z(z2[0], 1), move_z(z2[1], -1)
    a2, b2, z3 = lax.optimization_barrier((a2, b2, z3))
    pieces = [near_a, *a2, *far(*a2, along_x), near_b, *b2, *far(*b2, along_y)]
    z4 = far(*z3, move_z)
    right = jnp.concatenate([top_inv, *z1, *z2, *z3, *z4], axis=0)
    *pieces, right = lax.optimization_barrier((*pieces, right))
    return pieces, left, right


def exchange_z(a):
    groups = [[2 * z + c for z in range(ZS)] for c in range(CORES)]
    return lax.all_to_all(a, "snode", 0, 0, axis_index_groups=groups)


def gather_z(a):
    mine = exchange_z(jnp.broadcast_to(a[None], (ZS, *a.shape)))
    return mine, swap_core(mine)


def each_block(pieces, x, y, per):
    for half in range(2):
        group = pieces[5 * half : 5 * half + 5]
        for far in range(4):
            for near in range(4):
                if far < 3:
                    piece, at = group[far], near * per
                else:
                    piece, at = (group[3], near * per) if near < 2 else (group[4], (near - 2) * per)
                a, b = (OFFSETS[far], OFFSETS[near]) if half == 0 else (OFFSETS[near], OFFSETS[far])
                yield half, piece, at, lax.rem(x + a, 4), lax.rem(y + b, 4)


def forward_kernel(place, rows, loads, *refs):
    pieces, (inv, panel, forward, update, partial_value) = refs[:10], refs[10:]
    x, y = place[2], place[3]
    for half, piece, at, bx, by in each_block(pieces, x, y, 2):
        r = 4 * bx + by
        for leaf in range(2):
            inv[2 * half + leaf, pl.ds(pl.multiple_of(r * 32, 32), 32), :] = piece[at + leaf, :32, :]
            panel[2 * half + leaf, pl.ds(pl.multiple_of(r * 64, 64), 64), :] = piece[at + leaf, 32:, :]
    for leaf in range(4):
        value = jnp.dot(inv[leaf], loads[leaf], preferred_element_type=F32).astype(BF)
        forward[leaf] = value
        partial_value[leaf * 1024 : leaf * 1024 + 1024, :] = jnp.dot(
            panel[leaf], value, preferred_element_type=F32
        ).astype(BF)

    @pl.loop(0, 4)
    def _(block):
        total = None
        for k in range(8):
            target = rows[0:1, k * 512 : k * 512 + 512] - block * 1024
            hit = lax.broadcasted_iota(jnp.int32, (1024, 512), 0) == target
            term = jnp.dot(
                hit.astype(F32).astype(BF), partial_value[k * 512 : k * 512 + 512, :], preferred_element_type=F32
            )
            total = term if total is None else total + term
        update[pl.ds(pl.multiple_of(block * 1024, 1024), 1024), :] = total.astype(BF)


def square_kernel(place, after, left, right, right_other, out, total):
    z, c = place[0], place[1]
    for k, offset in enumerate(Z_OFFSETS):
        chip = lax.rem(z + offset, 8)
        for core, part in ((c, right), (1 - c, right_other)):
            first = pl.multiple_of((2 * chip + core) * 256, 256)
            total[pl.ds(first, 256), :] = part[k * 256 : k * 256 + 256, :]
    out[...] = lax.dot_general(
        left[...], total[...], (((0,), (0,)), ((), ())), preferred_element_type=F32
    ).astype(BF)


def top_kernel(place, reduced_mine, reduced_other, square, out, row_block, reduced):
    c = place[1]
    for k in range(16):
        row_block[:, k * 256 : k * 256 + 256] = square[k * 256 : k * 256 + 256, :]
    for k in range(8):
        reduced[pl.ds(pl.multiple_of((2 * k + c) * 256, 256), 256), :] = reduced_mine[k]
        reduced[pl.ds(pl.multiple_of((2 * k + 1 - c) * 256, 256), 256), :] = reduced_other[k]
    out[...] = jnp.dot(row_block[...], reduced[...], preferred_element_type=F32)


def backward_kernel(rows, inv, panel, forward, top_mine, top_other, out, top, picked):
    for k in range(8):
        top[k * 256 : k * 256 + 256, :] = top_mine[k].astype(F32)
        top[2048 + k * 256 : 2048 + k * 256 + 256, :] = top_other[k].astype(F32)
    for leaf in range(4):

        @pl.loop(0, 1024 // 16)
        def _(step):
            first = pl.multiple_of(step * 16, 16)
            found = [top[pl.ds(rows[leaf * 1024 + first + k], 1), :] for k in range(16)]
            picked[pl.ds(first, 16), :] = jnp.concatenate(found, axis=0).astype(BF)

        through = lax.dot_general(panel[leaf], picked[...], (((0,), (0,)), ((), ())), preferred_element_type=F32)
        value = (forward[leaf].astype(F32) - through).astype(BF)
        out[leaf] = lax.dot_general(inv[leaf], value, (((0,), (0,)), ((), ())), preferred_element_type=F32)


def per_device(leaf_inv, leaf_panel, leaf_rows, leaf_loads, top_inv, top_loads):
    s, r = lax.axis_index("snode"), lax.axis_index("rhs")
    z, c, x, y = s // 2, s % 2, r // 4, r % 4
    place = jnp.stack([z, c, x, y]).astype(jnp.int32)
    own_core = ((leaf_rows // 256) % 2) == c
    slots = (jnp.where(own_core, 0, 2048) + (leaf_rows // 512) * 256 + leaf_rows % 256).reshape(-1)

    factors = jnp.concatenate([leaf_inv, leaf_panel], axis=1)
    pieces, left, right = gather_factors(factors[:2], factors[2:], top_inv)
    right_other = swap_core(right)
    inv, panel, forward, update = pl.pallas_call(
        forward_kernel,
        out_shape=(
            jax.ShapeDtypeStruct((4, 512, 512), BF),
            jax.ShapeDtypeStruct((4, 1024, 512), BF),
            jax.ShapeDtypeStruct((4, 512, 256), BF),
            jax.ShapeDtypeStruct((4096, 256), BF),
        ),
        in_specs=[SMEM] + [VMEM] * 12,
        out_specs=[VMEM] * 4,
        scratch_shapes=[pltpu.VMEM((4096, 256), BF)],
        compiler_params=PARAMS,
        cost_estimate=pl.CostEstimate(flops=10**10, bytes_accessed=20 * 2**20, transcendentals=0),
        name="leaf_forward",
    )(place, jnp.broadcast_to(slots[None], (8, 4096)), leaf_loads, *pieces)

    square = pl.pallas_call(
        square_kernel,
        out_shape=jax.ShapeDtypeStruct((256, 256), BF),
        in_specs=[SMEM, ANY] + [VMEM] * 3,
        out_specs=VMEM,
        scratch_shapes=[pltpu.VMEM((4096, 256), BF)],
        compiler_params=PARAMS,
        cost_estimate=pl.CostEstimate(flops=10**9, bytes_accessed=6 * 2**20, transcendentals=0),
        name="top_square",
    )(place, forward, left, right, right_other)
    square_rows = lax.all_gather(square, "rhs", axis=0, tiled=True)

    update = update.reshape(2, 8, 256, 256)
    chip = (update[0].astype(F32) + swap_core(update[1]).astype(F32)).astype(BF)
    total = jnp.sum(exchange_z(chip).astype(F32), axis=0)
    reduced = (top_loads.astype(F32) - total).astype(BF)
    reduced_mine, reduced_other = gather_z(reduced)
    top_solution = pl.pallas_call(
        top_kernel,
        out_shape=jax.ShapeDtypeStruct((256, 256), F32),
        in_specs=[SMEM] + [VMEM] * 3,
        out_specs=VMEM,
        scratch_shapes=[pltpu.VMEM((256, 4096), BF), pltpu.VMEM((4096, 256), BF)],
        compiler_params=PARAMS,
        cost_estimate=pl.CostEstimate(flops=10**9, bytes_accessed=6 * 2**20, transcendentals=0),
        name="top_solve",
    )(place, reduced_mine, reduced_other, square_rows)
    top_mine, top_other = gather_z(top_solution.astype(BF))
    leaf_solution = pl.pallas_call(
        backward_kernel,
        out_shape=jax.ShapeDtypeStruct((4, 512, 256), F32),
        in_specs=[SMEM] + [VMEM] * 5,
        out_specs=VMEM,
        scratch_shapes=[pltpu.VMEM((4096, 256), F32), pltpu.VMEM((1024, 256), BF)],
        compiler_params=PARAMS,
        cost_estimate=pl.CostEstimate(flops=10**10, bytes_accessed=12 * 2**20, transcendentals=0),
        name="leaf_backward",
    )(slots, inv, panel, forward, top_mine, top_other)
    return leaf_solution, top_solution


def solution(mesh):
    return jax.shard_map(
        per_device,
        mesh=mesh,
        in_specs=(
            P("snode", "rhs", None),
            P("snode", "rhs", None),
            P("snode", None),
            P("snode", None, "rhs"),
            P("snode", "rhs"),
            P("snode", "rhs"),
        ),
        out_specs=(P("snode", None, "rhs"), P("snode", "rhs")),
        check_vma=False,
    )
```

profile of v0, /device:TPU:1, one launch (start us, length us, event | category | flops | bytes accessed | tf_op | source)
XLA Modules:
  0.0 250.9 jit_solution(11297113375366690604)
XLA Ops:
  7.2 0.0 all-gather.3.cloned.1.call-start
  7.2 2.5 %collective-permute-start.4 = (bf16[256,256]{1,0:T(8,128)(2,1)}, bf16[256,256]{1,0:T(8,128)(2,1)S(1)}, u32[]{:S(2)}, u32[]{:S(2)}) collective-permute-start(bf16[256,256]{1,0:T(8,128)(2,1)} %param.10), channel_id=1, source_target_pairs={{0,32},{16,48},{32,64},{48,80},{64,96},{80,112},{96,128},{112,144}... | collective-permute-start | bytes 393224 | tf_op jit(solution)/shard_map/ppermute | solution.py:25
  9.8 4.0 %collective-permute-start.5 = (bf16[256,256]{1,0:T(8,128)(2,1)}, bf16[256,256]{1,0:T(8,128)(2,1)S(1)}, u32[]{:S(2)}, u32[]{:S(2)}) collective-permute-start(bf16[256,256]{1,0:T(8,128)(2,1)} %param.10), channel_id=1, source_target_pairs={{0,224},{16,240},{32,0},{48,16},{64,32},{80,48},{96,64},{112,80},{... | collective-permute-start | bytes 393224 | tf_op jit(solution)/shard_map/ppermute | solution.py:25
  13.8 0.9 constant_dynamic-update-slice_fusion.1
  14.7 1.0 constant_dynamic-update-slice_fusion
  15.7 0.8 constant_dynamic-update-slice_fusion.11
  16.5 1.3 collective-permute-start
  17.8 1.4 collective-permute-start.1
  19.2 1.2 collective-permute-start.2
  20.5 1.5 collective-permute-start.3
  21.9 3.9 %collective-permute-start.6 = (bf16[256,256]{1,0:T(8,128)(2,1)}, bf16[256,256]{1,0:T(8,128)(2,1)S(1)}, u32[]{:S(2)}, u32[]{:S(2)}) collective-permute-start(bf16[256,256]{1,0:T(8,128)(2,1)} %param.10), channel_id=1, source_target_pairs={{0,0},{1,16},{2,32},{3,48},{4,64},{5,80},{6,96},{7,112},{8,128},{9... | collective-permute-start | bytes 393224 | tf_op jit(solution)/shard_map/ppermute | solution.py:50
  25.8 3.0 %collective-permute-done.6 = bf16[256,256]{1,0:T(8,128)(2,1)S(1)} collective-permute-done((bf16[256,256]{1,0:T(8,128)(2,1)}, bf16[256,256]{1,0:T(8,128)(2,1)S(1)}, u32[]{:S(2)}, u32[]{:S(2)}) %collective-permute-start.6) | collective-permute-done | bytes 131104 | tf_op jit(solution)/shard_map/ppermute | solution.py:50
  28.9 0.8 constant_dynamic-update-slice_fusion.5
  29.7 0.7 constant_dynamic-update-slice_fusion.9
  30.4 6.7 %collective-permute-start.11 = (bf16[1,96,512]{2,1,0:T(8,128)(2,1)S(1)}, bf16[1,96,512]{2,1,0:T(8,128)(2,1)S(1)}, u32[]{:S(2)}, u32[]{:S(2)}) collective-permute-start(bf16[1,96,512]{2,1,0:T(8,128)(2,1)S(1)} %slice.48), channel_id=1, source_target_pairs={{0,4},{1,5},{2,6},{3,7},{4,8},{5,9},{6,10},{7,11},{8,12},{9,13},{1... | collective-permute-start | bytes 294920 | tf_op jit(solution)/shard_map/ppermute | solution.py:21
  37.1 6.3 %collective-permute-start.12 = (bf16[1,96,512]{2,1,0:T(8,128)(2,1)S(1)}, bf16[1,96,512]{2,1,0:T(8,128)(2,1)S(1)}, u32[]{:S(2)}, u32[]{:S(2)}) collective-permute-start(bf16[1,96,512]{2,1,0:T(8,128)(2,1)S(1)} %slice.49), channel_id=1, source_target_pairs={{0,12},{1,13},{2,14},{3,15},{4,0},{5,1},{6,2},{7,3},{8,4},{9,5},{1... | collective-permute-start | bytes 294920 | tf_op jit(solution)/shard_map/ppermute | solution.py:21
  43.3 3.6 %collective-permute-start.8 = (bf16[1,96,512]{2,1,0:T(8,128)(2,1)S(1)}, bf16[1,96,512]{2,1,0:T(8,128)(2,1)S(1)}, u32[]{:S(2)}, u32[]{:S(2)}) collective-permute-start(bf16[1,96,512]{2,1,0:T(8,128)(2,1)S(1)} %slice.47), channel_id=1, source_target_pairs={{0,3},{1,0},{2,1},{3,2},{4,7},{5,4},{6,5},{7,6},{8,11},{9,8},{10,9... | collective-permute-start | bytes 294920 | tf_op jit(solution)/shard_map/ppermute | solution.py:21
  47.0 0.7 constant_dynamic-update-slice_fusion.4
  47.7 0.6 constant_dynamic-update-slice_fusion.8
  48.3 0.6 constant_dynamic-update-slice_fusion.7.refs_5_
  49.0 2.7 %collective-permute-start.14 = (bf16[8,96,512]{2,1,0:T(8,128)(2,1)}, bf16[8,96,512]{2,1,0:T(8,128)(2,1)}, u32[]{:S(2)}, u32[]{:S(2)}) collective-permute-start(bf16[8,96,512]{2,1,0:T(8,128)(2,1)} %constant_dynamic-update-slice_fusion.7.refs_5_), channel_id=1, source_target_pairs={{0,3},{1,0},{2,1},{3,2},{4,7},{5,4},{6,5},{7,6},{8,11},{9,8},{10,9... | collective-permute-start | bytes 2359304 | tf_op jit(solution)/shard_map/ppermute | solution.py:21
  51.6 0.6 constant_dynamic-update-slice_fusion.3
  52.3 0.6 constant_dynamic-update-slice_fusion.2.refs_0_
  52.9 1.5 collective-permute-start.10
  54.4 0.1 fusion.7
  54.5 4.5 %collective-permute-start.17 = (bf16[256,256]{1,0:T(8,128)(2,1)S(1)}, bf16[256,256]{1,0:T(8,128)(2,1)}, u32[]{:S(2)}, u32[]{:S(2)}) collective-permute-start(bf16[256,256]{1,0:T(8,128)(2,1)S(1)} %collective-permute-done.5), channel_id=1, source_target_pairs={{0,224},{16,240},{32,0},{48,16},{64,32},{80,48},{96,64},{112,80},{... | collective-permute-start | bytes 393224 | tf_op jit(solution)/shard_map/ppermute | solution.py:25
  59.0 0.1 pad_add_fusion.place
  59.1 1.9 collective-permute-done.17
  61.0 6.2 %collective-permute-done.16 = bf16[256,256]{1,0:T(8,128)(2,1)S(1)} collective-permute-done((bf16[256,256]{1,0:T(8,128)(2,1)S(1)}, bf16[256,256]{1,0:T(8,128)(2,1)S(1)}, u32[]{:S(2)}, u32[]{:S(2)}) %collective-permute-start.16) | collective-permute-done | bytes 131104 | tf_op jit(solution)/shard_map/ppermute | solution.py:25
  67.2 1.5 collective-permute-start.18
  68.7 0.9 constant_dynamic-update-slice_fusion.16
  69.6 1.9 collective-permute-done.18
  71.6 0.1 collective-permute-start.19
  71.7 2.7 %collective-permute-start.20 = (bf16[4,96,512]{2,1,0:T(8,128)(2,1)S(1)}, bf16[4,96,512]{2,1,0:T(8,128)(2,1)S(1)}, u32[]{:S(2)}, u32[]{:S(2)}) collective-permute-start(bf16[4,96,512]{2,1,0:T(8,128)(2,1)S(1)} %slice.51), channel_id=1, source_target_pairs={{0,12},{1,13},{2,14},{3,15},{4,0},{5,1},{6,2},{7,3},{8,4},{9,5},{1... | collective-permute-start | bytes 1179656 | tf_op jit(solution)/shard_map/ppermute | solution.py:21
  74.5 1.0 slice.52
  75.5 0.1 collective-permute-start.21
  75.6 1.0 slice.53
  76.6 2.7 %collective-permute-start.22 = (bf16[4,96,512]{2,1,0:T(8,128)(2,1)S(1)}, bf16[4,96,512]{2,1,0:T(8,128)(2,1)S(1)}, u32[]{:S(2)}, u32[]{:S(2)}) collective-permute-start(bf16[4,96,512]{2,1,0:T(8,128)(2,1)S(1)} %slice.53), channel_id=1, source_target_pairs={{0,3},{1,0},{2,1},{3,2},{4,7},{5,4},{6,5},{7,6},{8,11},{9,8},{10,9... | collective-permute-start | bytes 1179656 | tf_op jit(solution)/shard_map/ppermute | solution.py:21
  79.4 0.1 collective-permute-start.23
  79.5 6.3 %collective-permute-done.23 = bf16[128,256]{1,0:T(8,128)(2,1)S(1)} collective-permute-done((bf16[128,256]{1,0:T(8,128)(2,1)S(1)}, bf16[128,256]{1,0:T(8,128)(2,1)S(1)}, u32[]{:S(2)}, u32[]{:S(2)}) %collective-permute-start.23) | collective-permute-done | bytes 65568 | tf_op jit(solution)/shard_map/ppermute | solution.py:25
  85.8 1.4 collective-permute-start.24
  87.2 2.2 collective-permute-done.24
  89.4 15.3 %leaf_forward.1 = (bf16[4,512,512]{2,1,0:T(8,128)(2,1)}, bf16[4,1024,512]{2,1,0:T(8,128)(2,1)}, bf16[4,512,256]{2,1,0:T(8,128)(2,1)}, bf16[4096,256]{1,0:T(8,128)(2,1)}) custom-call(s32[4]{0:T(128)S(1)} %pad_add_fusion.place, s32[8,4096]{1,0:T(8,128)S(1)} %broadcast_in_dim.13.rows, bf16[4,512,256]{2,1,0:T(8,128)(2,1)} %loads.1, ...), custom_call_target="tpu_custom_call" | custom-call | flops 10000000000 | bytes 20971520 | tf_op jit(solution)/shard_map/leaf_forward/pallas_call | solution.py:168
  104.7 1.7 fusion.9
  106.4 6.5 %collective-permute-start.25 = (bf16[8,256,256]{2,1,0:T(8,128)(2,1)S(1)}, bf16[8,256,256]{2,1,0:T(8,128)(2,1)S(1)}, u32[]{:S(2)}, u32[]{:S(2)}) collective-permute-start(bf16[8,256,256]{2,1,0:T(8,128)(2,1)S(1)} %bitcast.15), channel_id=1, source_target_pairs={{0,16},{16,0},{32,48},{48,32},{64,80},{80,64},{96,112},{112,96},{1... | collective-permute-start | bytes 3145736 | tf_op jit(solution)/shard_map/ppermute | solution.py:29
  113.0 2.3 collective-permute-done.25
  115.3 1.3 fusion
  116.5 6.1 %all-to-all-start = ((bf16[8,256,256]{2,1,0:T(8,128)(2,1)}), bf16[8,256,256]{2,1,0:T(8,128)(2,1)}, u32[]{:S(2)}, u32[]{:S(2)}) async-start(bf16[8,256,256]{2,1,0:T(8,128)(2,1)} %fusion), calls=%async_computation | async-start | bytes 2097152 | tf_op jit(solution)/shard_map/all_to_all | solution.py:70
  122.6 1.0 collective-permute-start.27
  123.6 2.3 collective-permute-done.27.right_other
  125.9 3.2 %top_square.1 = bf16[256,256]{1,0:T(8,128)(2,1)} custom-call(s32[4]{0:T(128)S(1)} %pad_add_fusion.place, bf16[4,512,256]{2,1,0:T(8,128)(2,1)S(1)} %copy-done, bf16[4096,256]{1,0:T(8,128)(2,1)} %all-gather.3.cloned.1.call-done.left, bf16[2048,256]{1,0:T(8,128)(2,1)S(1)} %constant_dynamic-update-slice_fusion.12.right, ...), custom_call_target="tpu_custom_call" | custom-call | flops 1000000000 | bytes 6291456 | tf_op jit(solution)/shard_map/top_square/pallas_call | solution.py:184
  129.1 22.9 %all-to-all-done = bf16[8,256,256]{2,1,0:T(8,128)(2,1)} async-done(((bf16[8,256,256]{2,1,0:T(8,128)(2,1)}), bf16[8,256,256]{2,1,0:T(8,128)(2,1)}, u32[]{:S(2)}, u32[]{:S(2)}) %all-to-all-start) | async-done | bytes 1048608 | tf_op jit(solution)/shard_map/all_to_all | solution.py:70
  151.9 1.4 convert_reduce_fusion
  153.4 0.1 broadcast_in_dim.14
  153.4 31.4 %all_to_all.15.reduced_mine = bf16[8,256,256]{2,1,0:T(8,128)(2,1)S(1)} all-to-all(bf16[8,256,256]{2,1,0:T(8,128)(2,1)S(1)} %broadcast_in_dim.14), channel_id=1, replica_groups={{0,32,64,96,128,160,192,224},{16,48,80,112,144,176,208,240},{1,33,65,97..., dimensions={0} | all-to-all | bytes 2097152 | tf_op jit(solution)/shard_map/all_to_all | solution.py:70
  184.8 0.7 collective-permute-start.26
  185.5 2.3 collective-permute-done.26.reduced_other
  187.8 3.1 %top_solve.1 = f32[256,256]{1,0:T(8,128)} custom-call(s32[4]{0:T(128)S(1)} %pad_add_fusion.place, bf16[8,256,256]{2,1,0:T(8,128)(2,1)S(1)} %all_to_all.15.reduced_mine, bf16[8,256,256]{2,1,0:T(8,128)(2,1)S(1)} %collective-permute-done.26.reduced_other, bf16[4096,256]{1,0:T(8,128)(2,1)} %all-gather.5.cloned.1.call-done.square), custom_call_target="tpu_custom_call" | custom-call | flops 1000000000 | bytes 6291456 | tf_op jit(solution)/shard_map/top_solve/pallas_call | solution.py:201
  191.0 1.0 convert_element_type.31
  191.9 0.1 broadcast_in_dim.26
  192.0 31.6 %all_to_all.16.top_mine = bf16[8,256,256]{2,1,0:T(8,128)(2,1)S(1)} all-to-all(bf16[8,256,256]{2,1,0:T(8,128)(2,1)S(1)} %broadcast_in_dim.26), channel_id=1, replica_groups={{0,32,64,96,128,160,192,224},{16,48,80,112,144,176,208,240},{1,33,65,97..., dimensions={0} | all-to-all | bytes 2097152 | tf_op jit(solution)/shard_map/all_to_all | solution.py:70
  223.6 0.5 collective-permute-start.28
  224.1 2.3 collective-permute-done.28.top_other
  226.4 17.6 %leaf_backward.1 = f32[4,512,256]{2,1,0:T(8,128)} custom-call(s32[4096]{0:T(1024)S(1)} %bitcast.13, bf16[4,512,512]{2,1,0:T(8,128)(2,1)} %get-tuple-element.52.inv, bf16[4,1024,512]{2,1,0:T(8,128)(2,1)} %get-tuple-element.53.panel, bf16[4,512,256]{2,1,0:T(8,128)(2,1)S(1)} %copy-done, bf16[8,256,256]{2,1,0:T(8,128)(2,1)S(1)} %all_to_all.16.top_mine, ...), custom_call_target="tpu_custom_call" | custom-call | flops 10000000000 | bytes 12582912 | tf_op jit(solution)/shard_map/leaf_backward/pallas_call | solution.py:212
  (58 shorter events, 0.4 us)
Async XLA Ops:
  7.2 118.7 %all-gather.3.cloned.1.call-start = ((), (), s32[]{:S(2)}) async-start(), calls=%async_computation.3 | async-start | bytes 2228224 | tf_op jit(solution)/shard_map/all_gather | solution.py:54
  7.2 13.3 %collective-permute-start.4 = (bf16[256,256]{1,0:T(8,128)(2,1)}, bf16[256,256]{1,0:T(8,128)(2,1)S(1)}, u32[]{:S(2)}, u32[]{:S(2)}) collective-permute-start(bf16[256,256]{1,0:T(8,128)(2,1)} %param.10), channel_id=1, source_target_pairs={{0,32},{16,48},{32,64},{48,80},{64,96},{80,112},{96,128},{112,144}... | collective-permute-start | bytes 393224 | tf_op jit(solution)/shard_map/ppermute | solution.py:25
  9.8 12.2 %collective-permute-start.5 = (bf16[256,256]{1,0:T(8,128)(2,1)}, bf16[256,256]{1,0:T(8,128)(2,1)S(1)}, u32[]{:S(2)}, u32[]{:S(2)}) collective-permute-start(bf16[256,256]{1,0:T(8,128)(2,1)} %param.10), channel_id=1, source_target_pairs={{0,224},{16,240},{32,0},{48,16},{64,32},{80,48},{96,64},{112,80},{... | collective-permute-start | bytes 393224 | tf_op jit(solution)/shard_map/ppermute | solution.py:25
  15.7 38.7 %copy-start.4 = (s32[4,1024]{1,0:T(4,128)S(1)}, s32[4,1024]{1,0:T(4,128)}, u32[]{:S(2)}) copy-start(s32[4,1024]{1,0:T(4,128)} %param.8) | copy-start | bytes 49156
  15.7 43.4 %copy-start.1 = (bf16[256,256]{1,0:T(8,128)(2,1)S(1)}, bf16[256,256]{1,0:T(8,128)(2,1)}, u32[]{:S(2)}) copy-start(bf16[256,256]{1,0:T(8,128)(2,1)} %param.10) | copy-start | bytes 393220
  16.5 12.3 %collective-permute-start = (bf16[2,96,512]{2,1,0:T(8,128)(2,1)S(1)}, bf16[2,96,512]{2,1,0:T(8,128)(2,1)S(1)}, u32[]{:S(2)}, u32[]{:S(2)}) collective-permute-start(bf16[2,96,512]{2,1,0:T(8,128)(2,1)S(1)} %get-tuple-element.63), channel_id=1, source_target_pairs={{0,1},{1,2},{2,3},{3,0},{4,5},{5,6},{6,7},{7,4},{8,9},{9,10},{10,1... | collective-permute-start | bytes 589832 | tf_op jit(solution)/shard_map/ppermute | solution.py:21
  17.8 11.0 %collective-permute-start.1 = (bf16[2,96,512]{2,1,0:T(8,128)(2,1)S(1)}, bf16[2,96,512]{2,1,0:T(8,128)(2,1)S(1)}, u32[]{:S(2)}, u32[]{:S(2)}) collective-permute-start(bf16[2,96,512]{2,1,0:T(8,128)(2,1)S(1)} %get-tuple-element.63), channel_id=1, source_target_pairs={{0,3},{1,0},{2,1},{3,2},{4,7},{5,4},{6,5},{7,6},{8,11},{9,8},{10,9... | collective-permute-start | bytes 589832 | tf_op jit(solution)/shard_map/ppermute | solution.py:21
  19.2 9.6 %collective-permute-start.2 = (bf16[2,96,512]{2,1,0:T(8,128)(2,1)S(1)}, bf16[2,96,512]{2,1,0:T(8,128)(2,1)S(1)}, u32[]{:S(2)}, u32[]{:S(2)}) collective-permute-start(bf16[2,96,512]{2,1,0:T(8,128)(2,1)S(1)} %get-tuple-element.62), channel_id=1, source_target_pairs={{0,4},{1,5},{2,6},{3,7},{4,8},{5,9},{6,10},{7,11},{8,12},{9,13},{1... | collective-permute-start | bytes 589832 | tf_op jit(solution)/shard_map/ppermute | solution.py:21
  20.5 8.4 %collective-permute-start.3 = (bf16[2,96,512]{2,1,0:T(8,128)(2,1)S(1)}, bf16[2,96,512]{2,1,0:T(8,128)(2,1)S(1)}, u32[]{:S(2)}, u32[]{:S(2)}) collective-permute-start(bf16[2,96,512]{2,1,0:T(8,128)(2,1)S(1)} %get-tuple-element.62), channel_id=1, source_target_pairs={{0,12},{1,13},{2,14},{3,15},{4,0},{5,1},{6,2},{7,3},{8,4},{9,5},{1... | collective-permute-start | bytes 589832 | tf_op jit(solution)/shard_map/ppermute | solution.py:21
  21.9 6.9 %collective-permute-start.6 = (bf16[256,256]{1,0:T(8,128)(2,1)}, bf16[256,256]{1,0:T(8,128)(2,1)S(1)}, u32[]{:S(2)}, u32[]{:S(2)}) collective-permute-start(bf16[256,256]{1,0:T(8,128)(2,1)} %param.10), channel_id=1, source_target_pairs={{0,0},{1,16},{2,32},{3,48},{4,64},{5,80},{6,96},{7,112},{8,128},{9... | collective-permute-start | bytes 393224 | tf_op jit(solution)/shard_map/ppermute | solution.py:50
  28.8 32.2 %copy-start.2 = (bf16[256,256]{1,0:T(8,128)(2,1)}, bf16[256,256]{1,0:T(8,128)(2,1)S(1)}, u32[]{:S(2)}) copy-start(bf16[256,256]{1,0:T(8,128)(2,1)S(1)} %collective-permute-done.6) | copy-start | bytes 393220
  30.4 17.3 %collective-permute-start.11 = (bf16[1,96,512]{2,1,0:T(8,128)(2,1)S(1)}, bf16[1,96,512]{2,1,0:T(8,128)(2,1)S(1)}, u32[]{:S(2)}, u32[]{:S(2)}) collective-permute-start(bf16[1,96,512]{2,1,0:T(8,128)(2,1)S(1)} %slice.48), channel_id=1, source_target_pairs={{0,4},{1,5},{2,6},{3,7},{4,8},{5,9},{6,10},{7,11},{8,12},{9,13},{1... | collective-permute-start | bytes 294920 | tf_op jit(solution)/shard_map/ppermute | solution.py:21
  37.1 11.2 %collective-permute-start.12 = (bf16[1,96,512]{2,1,0:T(8,128)(2,1)S(1)}, bf16[1,96,512]{2,1,0:T(8,128)(2,1)S(1)}, u32[]{:S(2)}, u32[]{:S(2)}) collective-permute-start(bf16[1,96,512]{2,1,0:T(8,128)(2,1)S(1)} %slice.49), channel_id=1, source_target_pairs={{0,12},{1,13},{2,14},{3,15},{4,0},{5,1},{6,2},{7,3},{8,4},{9,5},{1... | collective-permute-start | bytes 294920 | tf_op jit(solution)/shard_map/ppermute | solution.py:21
  43.3 8.3 %collective-permute-start.7 = (bf16[1,96,512]{2,1,0:T(8,128)(2,1)S(1)}, bf16[1,96,512]{2,1,0:T(8,128)(2,1)S(1)}, u32[]{:S(2)}, u32[]{:S(2)}) collective-permute-start(bf16[1,96,512]{2,1,0:T(8,128)(2,1)S(1)} %slice.46), channel_id=1, source_target_pairs={{0,1},{1,2},{2,3},{3,0},{4,5},{5,6},{6,7},{7,4},{8,9},{9,10},{10,1... | collective-permute-start | bytes 294920 | tf_op jit(solution)/shard_map/ppermute | solution.py:21
  43.3 8.9 %collective-permute-start.8 = (bf16[1,96,512]{2,1,0:T(8,128)(2,1)S(1)}, bf16[1,96,512]{2,1,0:T(8,128)(2,1)S(1)}, u32[]{:S(2)}, u32[]{:S(2)}) collective-permute-start(bf16[1,96,512]{2,1,0:T(8,128)(2,1)S(1)} %slice.47), channel_id=1, source_target_pairs={{0,3},{1,0},{2,1},{3,2},{4,7},{5,4},{6,5},{7,6},{8,11},{9,8},{10,9... | collective-permute-start | bytes 294920 | tf_op jit(solution)/shard_map/ppermute | solution.py:21
  47.0 7.5 %collective-permute-start.15 = (bf16[256,256]{1,0:T(8,128)(2,1)S(1)}, bf16[256,256]{1,0:T(8,128)(2,1)S(1)}, u32[]{:S(2)}, u32[]{:S(2)}) collective-permute-start(bf16[256,256]{1,0:T(8,128)(2,1)S(1)} %collective-permute-done.4), channel_id=1, source_target_pairs={{0,32},{16,48},{32,64},{48,80},{64,96},{80,112},{96,128},{112,144}... | collective-permute-start | bytes 393224 | tf_op jit(solution)/shard_map/ppermute | solution.py:25
  49.0 22.6 %collective-permute-start.13 = (bf16[8,96,512]{2,1,0:T(8,128)(2,1)}, bf16[8,96,512]{2,1,0:T(8,128)(2,1)}, u32[]{:S(2)}, u32[]{:S(2)}) collective-permute-start(bf16[8,96,512]{2,1,0:T(8,128)(2,1)} %constant_dynamic-update-slice_fusion.7.refs_5_), channel_id=1, source_target_pairs={{0,1},{1,2},{2,3},{3,0},{4,5},{5,6},{6,7},{7,4},{8,9},{9,10},{10,1... | collective-permute-start | bytes 2359304 | tf_op jit(solution)/shard_map/ppermute | solution.py:21
  49.0 22.6 %collective-permute-start.14 = (bf16[8,96,512]{2,1,0:T(8,128)(2,1)}, bf16[8,96,512]{2,1,0:T(8,128)(2,1)}, u32[]{:S(2)}, u32[]{:S(2)}) collective-permute-start(bf16[8,96,512]{2,1,0:T(8,128)(2,1)} %constant_dynamic-update-slice_fusion.7.refs_5_), channel_id=1, source_target_pairs={{0,3},{1,0},{2,1},{3,2},{4,7},{5,4},{6,5},{7,6},{8,11},{9,8},{10,9... | collective-permute-start | bytes 2359304 | tf_op jit(solution)/shard_map/ppermute | solution.py:21
  52.9 18.6 %collective-permute-start.10 = (bf16[8,96,512]{2,1,0:T(8,128)(2,1)}, bf16[8,96,512]{2,1,0:T(8,128)(2,1)S(1)}, u32[]{:S(2)}, u32[]{:S(2)}) collective-permute-start(bf16[8,96,512]{2,1,0:T(8,128)(2,1)} %constant_dynamic-update-slice_fusion.2.refs_0_), channel_id=1, source_target_pairs={{0,12},{1,13},{2,14},{3,15},{4,0},{5,1},{6,2},{7,3},{8,4},{9,5},{1... | collective-permute-start | bytes 2359304 | tf_op jit(solution)/shard_map/ppermute | solution.py:21
  54.4 17.2 %collective-permute-start.9 = (bf16[8,96,512]{2,1,0:T(8,128)(2,1)}, bf16[8,96,512]{2,1,0:T(8,128)(2,1)S(1)}, u32[]{:S(2)}, u32[]{:S(2)}) collective-permute-start(bf16[8,96,512]{2,1,0:T(8,128)(2,1)} %constant_dynamic-update-slice_fusion.2.refs_0_), channel_id=1, source_target_pairs={{0,4},{1,5},{2,6},{3,7},{4,8},{5,9},{6,10},{7,11},{8,12},{9,13},{1... | collective-permute-start | bytes 2359304 | tf_op jit(solution)/shard_map/ppermute | solution.py:21
  54.5 6.5 %collective-permute-start.17 = (bf16[256,256]{1,0:T(8,128)(2,1)S(1)}, bf16[256,256]{1,0:T(8,128)(2,1)}, u32[]{:S(2)}, u32[]{:S(2)}) collective-permute-start(bf16[256,256]{1,0:T(8,128)(2,1)S(1)} %collective-permute-done.5), channel_id=1, source_target_pairs={{0,224},{16,240},{32,0},{48,16},{64,32},{80,48},{96,64},{112,80},{... | collective-permute-start | bytes 393224 | tf_op jit(solution)/shard_map/ppermute | solution.py:25
  61.0 6.2 %collective-permute-start.16 = (bf16[256,256]{1,0:T(8,128)(2,1)S(1)}, bf16[256,256]{1,0:T(8,128)(2,1)S(1)}, u32[]{:S(2)}, u32[]{:S(2)}) collective-permute-start(bf16[256,256]{1,0:T(8,128)(2,1)S(1)} %collective-permute-done.15), channel_id=1, source_target_pairs={{0,32},{16,48},{32,64},{48,80},{64,96},{80,112},{96,128},{112,144}... | collective-permute-start | bytes 393224 | tf_op jit(solution)/shard_map/ppermute | solution.py:25
  67.2 4.3 %collective-permute-start.18 = (bf16[256,256]{1,0:T(8,128)(2,1)}, bf16[256,256]{1,0:T(8,128)(2,1)S(1)}, u32[]{:S(2)}, u32[]{:S(2)}) collective-permute-start(bf16[256,256]{1,0:T(8,128)(2,1)} %collective-permute-done.17), channel_id=1, source_target_pairs={{0,224},{16,240},{32,0},{48,16},{64,32},{80,48},{96,64},{112,80},{... | collective-permute-start | bytes 393224 | tf_op jit(solution)/shard_map/ppermute | solution.py:25
  71.6 17.7 %collective-permute-start.19 = (bf16[4,96,512]{2,1,0:T(8,128)(2,1)S(1)}, bf16[4,96,512]{2,1,0:T(8,128)(2,1)S(1)}, u32[]{:S(2)}, u32[]{:S(2)}) collective-permute-start(bf16[4,96,512]{2,1,0:T(8,128)(2,1)S(1)} %slice.50), channel_id=1, source_target_pairs={{0,4},{1,5},{2,6},{3,7},{4,8},{5,9},{6,10},{7,11},{8,12},{9,13},{1... | collective-permute-start | bytes 1179656 | tf_op jit(solution)/shard_map/ppermute | solution.py:21
  71.7 17.6 %collective-permute-start.20 = (bf16[4,96,512]{2,1,0:T(8,128)(2,1)S(1)}, bf16[4,96,512]{2,1,0:T(8,128)(2,1)S(1)}, u32[]{:S(2)}, u32[]{:S(2)}) collective-permute-start(bf16[4,96,512]{2,1,0:T(8,128)(2,1)S(1)} %slice.51), channel_id=1, source_target_pairs={{0,12},{1,13},{2,14},{3,15},{4,0},{5,1},{6,2},{7,3},{8,4},{9,5},{1... | collective-permute-start | bytes 1179656 | tf_op jit(solution)/shard_map/ppermute | solution.py:21
  75.5 13.9 %collective-permute-start.21 = (bf16[4,96,512]{2,1,0:T(8,128)(2,1)S(1)}, bf16[4,96,512]{2,1,0:T(8,128)(2,1)S(1)}, u32[]{:S(2)}, u32[]{:S(2)}) collective-permute-start(bf16[4,96,512]{2,1,0:T(8,128)(2,1)S(1)} %slice.52), channel_id=1, source_target_pairs={{0,1},{1,2},{2,3},{3,0},{4,5},{5,6},{6,7},{7,4},{8,9},{9,10},{10,1... | collective-permute-start | bytes 1179656 | tf_op jit(solution)/shard_map/ppermute | solution.py:21
  76.6 12.8 %collective-permute-start.22 = (bf16[4,96,512]{2,1,0:T(8,128)(2,1)S(1)}, bf16[4,96,512]{2,1,0:T(8,128)(2,1)S(1)}, u32[]{:S(2)}, u32[]{:S(2)}) collective-permute-start(bf16[4,96,512]{2,1,0:T(8,128)(2,1)S(1)} %slice.53), channel_id=1, source_target_pairs={{0,3},{1,0},{2,1},{3,2},{4,7},{5,4},{6,5},{7,6},{8,11},{9,8},{10,9... | collective-permute-start | bytes 1179656 | tf_op jit(solution)/shard_map/ppermute | solution.py:21
  79.4 6.4 %collective-permute-start.23 = (bf16[128,256]{1,0:T(8,128)(2,1)S(1)}, bf16[128,256]{1,0:T(8,128)(2,1)S(1)}, u32[]{:S(2)}, u32[]{:S(2)}) collective-permute-start(bf16[128,256]{1,0:T(8,128)(2,1)S(1)} %slice.54), channel_id=1, source_target_pairs={{0,32},{16,48},{32,64},{48,80},{64,96},{80,112},{96,128},{112,144}... | collective-permute-start | bytes 196616 | tf_op jit(solution)/shard_map/ppermute | solution.py:25
  85.8 3.5 %collective-permute-start.24 = (bf16[128,256]{1,0:T(8,128)(2,1)S(1)}, bf16[128,256]{1,0:T(8,128)(2,1)S(1)}, u32[]{:S(2)}, u32[]{:S(2)}) collective-permute-start(bf16[128,256]{1,0:T(8,128)(2,1)S(1)} %slice.55), channel_id=1, source_target_pairs={{0,224},{16,240},{32,0},{48,16},{64,32},{80,48},{96,64},{112,80},{... | collective-permute-start | bytes 196616 | tf_op jit(solution)/shard_map/ppermute | solution.py:25
  106.4 8.8 %collective-permute-start.25 = (bf16[8,256,256]{2,1,0:T(8,128)(2,1)S(1)}, bf16[8,256,256]{2,1,0:T(8,128)(2,1)S(1)}, u32[]{:S(2)}, u32[]{:S(2)}) collective-permute-start(bf16[8,256,256]{2,1,0:T(8,128)(2,1)S(1)} %bitcast.15), channel_id=1, source_target_pairs={{0,16},{16,0},{32,48},{48,32},{64,80},{80,64},{96,112},{112,96},{1... | collective-permute-start | bytes 3145736 | tf_op jit(solution)/shard_map/ppermute | solution.py:29
  115.3 10.6 %copy-start = (bf16[4,512,256]{2,1,0:T(8,128)(2,1)S(1)}, bf16[4,512,256]{2,1,0:T(8,128)(2,1)}, u32[]{:S(2)}) copy-start(bf16[4,512,256]{2,1,0:T(8,128)(2,1)} %get-tuple-element.54.after.forward) | copy-start | bytes 3145732
  116.5 35.4 %all-to-all-start = ((bf16[8,256,256]{2,1,0:T(8,128)(2,1)}), bf16[8,256,256]{2,1,0:T(8,128)(2,1)}, u32[]{:S(2)}, u32[]{:S(2)}) async-start(bf16[8,256,256]{2,1,0:T(8,128)(2,1)} %fusion), calls=%async_computation | async-start | bytes 2097152 | tf_op jit(solution)/shard_map/all_to_all | solution.py:70
  122.6 65.2 %all-gather.5.cloned.1.call-start = ((), (), s32[]{:S(2)}) async-start(), calls=%async_computation.4 | async-start | bytes 2228224 | tf_op jit(solution)/shard_map/all_gather | solution.py:194
  122.6 3.2 %collective-permute-start.27 = (bf16[2048,256]{1,0:T(8,128)(2,1)S(1)}, bf16[2048,256]{1,0:T(8,128)(2,1)S(1)}, u32[]{:S(2)}, u32[]{:S(2)}) collective-permute-start(bf16[2048,256]{1,0:T(8,128)(2,1)S(1)} %constant_dynamic-update-slice_fusion.12.right), channel_id=1, source_target_pairs={{0,16},{16,0},{32,48},{48,32},{64,80},{80,64},{96,112},{112,96},{1... | collective-permute-start | bytes 3145736 | tf_op jit(solution)/shard_map/ppermute | solution.py:29
  125.9 27.4 %copy-start.3 = (bf16[256,256]{1,0:T(8,128)(2,1)S(1)}, bf16[256,256]{1,0:T(8,128)(2,1)}, u32[]{:S(2)}) copy-start(bf16[256,256]{1,0:T(8,128)(2,1)} %param.11) | copy-start | bytes 393220
  184.8 3.0 %collective-permute-start.26 = (bf16[8,256,256]{2,1,0:T(8,128)(2,1)S(1)}, bf16[8,256,256]{2,1,0:T(8,128)(2,1)S(1)}, u32[]{:S(2)}, u32[]{:S(2)}) collective-permute-start(bf16[8,256,256]{2,1,0:T(8,128)(2,1)S(1)} %all_to_all.15.reduced_mine), channel_id=1, source_target_pairs={{0,16},{16,0},{32,48},{48,32},{64,80},{80,64},{96,112},{112,96},{1... | collective-permute-start | bytes 3145736 | tf_op jit(solution)/shard_map/ppermute | solution.py:29
  223.6 2.8 %collective-permute-start.28 = (bf16[8,256,256]{2,1,0:T(8,128)(2,1)S(1)}, bf16[8,256,256]{2,1,0:T(8,128)(2,1)S(1)}, u32[]{:S(2)}, u32[]{:S(2)}) collective-permute-start(bf16[8,256,256]{2,1,0:T(8,128)(2,1)S(1)} %all_to_all.16.top_mine), channel_id=1, source_target_pairs={{0,16},{16,0},{32,48},{48,32},{64,80},{80,64},{96,112},{112,96},{1... | collective-permute-start | bytes 3145736 | tf_op jit(solution)/shard_map/ppermute | solution.py:29
Sparse Core Ops, SparseCore 0:
  61.1 51.9 all-gather.2
  129.2 45.0 all-gather.4
where the time goes:
time: 251 us
  starting transfers between devices  64.5 us (26%)
  blocking collectives  63 us (25%)
  waiting for transfers between devices  53.5 us (21%)
  Pallas kernels  39.2 us (16%)
  between operations  14.4 us (6%)
  local copies, waits for them, and re-layouts  12.5 us (5%)
  other arithmetic  3.79 us (2%)
    all_to_all x2, blocking collectives, exchange_z(): return lax.all_to_all(a, 'snode', 0, 0, axis_index_groups=groups)  63 us
    ppermute x16, starting transfers between devices, move_rhs(): return lax.ppermute(a, 'rhs', pairs)  31.7 us
    all_to_all x1, waiting for transfers between devices, exchange_z(): return lax.all_to_all(a, 'snode', 0, 0, axis_index_groups=groups)  22.9 us
    ppermute x8, waiting for transfers between devices, move_z(): return lax.ppermute(a, 'snode', [(i, (i + 2 * d) % 16) for i in range(16)])  18.4 us
    pallas_call x1, Pallas kernels, per_device(): pl.pallas_call(backward_kernel, out_shape=jax.ShapeDtypeStruct((4, 512, 2...  17.6 us
    pallas_call x1, Pallas kernels, per_device(): pl.pallas_call(forward_kernel, out_shape=(jax.ShapeDtypeStruct((4, 512, 5...  15.3 us
    ppermute x8, starting transfers between devices, move_z(): return lax.ppermute(a, 'snode', [(i, (i + 2 * d) % 16) for i in range(16)])  14 us
    ppermute x4, waiting for transfers between devices, swap_core(): return lax.ppermute(a, 'snode', [(i, i ^ 1) for i in range(16)])  9.15 us
  transfers between devices with their start and end apart: 32, of which 11 were waited for; matrix products, arithmetic and copies ran while one was open for 5% of the time, Pallas kernels for 7%

commit v1 on v0

--- a/solution.py
+++ b/solution.py
@@ -8,8 +8,8 @@
 BF = jnp.bfloat16
 F32 = jnp.float32
 OFFSETS = (0, 3, 1, 2)
-Z_OFFSETS = (0, 7, 1, 6, 2, 5, 3, 4)
-ZS, XS, YS, CORES = 8, 4, 4, 2
+XS, YS = 4, 4
+Z_GROUPS = [[2 * z + c for z in range(8)] for c in range(2)]
 VMEM = pl.BlockSpec(memory_space=pltpu.VMEM)
 ANY = pl.BlockSpec(memory_space=pl.ANY)
 SMEM = pl.BlockSpec(memory_space=pltpu.SMEM)
@@ -21,10 +21,6 @@
     return lax.ppermute(a, "rhs", pairs)
 
 
-def move_z(a, d):
-    return lax.ppermute(a, "snode", [(i, (i + 2 * d) % 16) for i in range(16)])
-
-
 def swap_core(a):
     return lax.ppermute(a, "snode", [(i, i ^ 1) for i in range(16)])
 
@@ -49,30 +45,52 @@
 def gather_factors(first, second, top_inv):
     across = lax.ppermute(top_inv, ("snode", "rhs"), [(16 * a + b, 16 * b + a) for a in range(16) for b in range(16)])
     a1, b1 = around(first, along_y), around(second, along_x)
-    z1 = around(top_inv, move_z)
-    a1, b1, z1, across = lax.optimization_barrier((a1, b1, z1, across))
-    left = lax.all_gather(across, "rhs", axis=0, tiled=True)
     near_a = jnp.concatenate([first, *a1, *far(*a1, along_y)], axis=0)
     near_b = jnp.concatenate([second, *b1, *far(*b1, along_x)], axis=0)
+    near_a, near_b, across = lax.optimization_barrier((near_a, near_b, across))
     a2, b2 = around(near_a, along_x), around(near_b, along_y)
-    z2 = move_z(z1[0], 1), move_z(z1[1], -1)
-    z3 = move_z(z2[0], 1), move_z(z2[1], -1)
-    a2, b2, z3 = lax.optimization_barrier((a2, b2, z3))
-    pieces = [near_a, *a2, *far(*a2, along_x), near_b, *b2, *far(*b2, along_y)]
-    z4 = far(*z3, move_z)
-    right = jnp.concatenate([top_inv, *z1, *z2, *z3, *z4], axis=0)
-    *pieces, right = lax.optimization_barrier((*pieces, right))
-    return pieces, left, right
+    return [near_a, *a2, *far(*a2, along_x), near_b, *b2, *far(*b2, along_y)], across
 
 
 def exchange_z(a):
-    groups = [[2 * z + c for z in range(ZS)] for c in range(CORES)]
-    return lax.all_to_all(a, "snode", 0, 0, axis_index_groups=groups)
+    return lax.all_to_all(a, "snode", 0, 0, axis_index_groups=Z_GROUPS)
 
 
 def gather_z(a):
-    mine = exchange_z(jnp.broadcast_to(a[None], (ZS, *a.shape)))
-    return mine, swap_core(mine)
+    def onward(b, d):
+        pairs = [(i, (i + 2 * d) % 16 if i % 2 == 0 else (i - 2 * d) % 16) for i in range(16)]
+        return lax.ppermute(b, "snode", pairs)
+
+    rows = a.shape[0]
+    chip = jnp.concatenate([a, swap_core(a)], axis=0)
+    second = onward(chip, 2)
+    first = onward(chip, 1)
+    third = onward(second, 1)
+    fourth = onward(second[:rows], 2)
+    side = jnp.concatenate([first, second, third, fourth], axis=0)
+    return chip, side, swap_core(side)
+
+
+def gathered_blocks(z, c):
+    up = 1 - 2 * c
+    yield 0, 0, z, c
+    yield 0, 256, z, 1 - c
+    for d in (1, 2, 3):
+        below, above = lax.rem(z - d * up + 8, 8), lax.rem(z + d * up + 8, 8)
+        yield 1, (d - 1) * 512, below, c
+        yield 1, (d - 1) * 512 + 256, below, 1 - c
+        yield 2, (d - 1) * 512, above, 1 - c
+        yield 2, (d - 1) * 512 + 256, above, c
+    yield 1, 1536, lax.rem(z + 4, 8), c
+    yield 2, 1536, lax.rem(z + 4, 8), 1 - c
+
+
+def gathered_slot(chip, own_core, z, c):
+    ahead = jnp.where(c == 0, chip - z, z - chip) % 8
+    own, away = jnp.where(own_core, 0, 256), jnp.where(own_core, 256, 0)
+    middle = jnp.where(own_core, 512 + 1536, 2304 + 1536)
+    slot = jnp.where(ahead < 4, 2304 + (ahead - 1) * 512 + away, 512 + (7 - ahead) * 512 + own)
+    return jnp.where(ahead == 0, own, jnp.where(ahead == 4, middle, slot))
 
 
 def each_block(pieces, x, y, per):
@@ -117,31 +135,31 @@
 
 
 def square_kernel(place, after, left, right, right_other, out, total):
-    z, c = place[0], place[1]
-    for k, offset in enumerate(Z_OFFSETS):
-        chip = lax.rem(z + offset, 8)
+    c = place[1]
+    for chip in range(8):
         for core, part in ((c, right), (1 - c, right_other)):
             first = pl.multiple_of((2 * chip + core) * 256, 256)
-            total[pl.ds(first, 256), :] = part[k * 256 : k * 256 + 256, :]
+            total[pl.ds(first, 256), :] = part[chip * 256 : chip * 256 + 256, :]
     out[...] = lax.dot_general(
         left[...], total[...], (((0,), (0,)), ((), ())), preferred_element_type=F32
     ).astype(BF)
 
 
-def top_kernel(place, reduced_mine, reduced_other, square, out, row_block, reduced):
-    c = place[1]
+def top_kernel(place, own_chip, side, side_other, square, out, row_block, reduced):
+    z, c = place[0], place[1]
     for k in range(16):
         row_block[:, k * 256 : k * 256 + 256] = square[k * 256 : k * 256 + 256, :]
-    for k in range(8):
-        reduced[pl.ds(pl.multiple_of((2 * k + c) * 256, 256), 256), :] = reduced_mine[k]
-        reduced[pl.ds(pl.multiple_of((2 * k + 1 - c) * 256, 256), 256), :] = reduced_other[k]
+    pieces = (own_chip, side, side_other)
+    for piece, at, chip, core in gathered_blocks(z, c):
+        first = pl.multiple_of((2 * chip + core) * 256, 256)
+        reduced[pl.ds(first, 256), :] = pieces[piece][at : at + 256, :]
     out[...] = jnp.dot(row_block[...], reduced[...], preferred_element_type=F32)
 
 
-def backward_kernel(rows, inv, panel, forward, top_mine, top_other, out, top, picked):
-    for k in range(8):
-        top[k * 256 : k * 256 + 256, :] = top_mine[k].astype(F32)
-        top[2048 + k * 256 : 2048 + k * 256 + 256, :] = top_other[k].astype(F32)
+def backward_kernel(rows, inv, panel, forward, own_chip, side, side_other, out, top, picked):
+    top[:512, :] = own_chip[...].astype(F32)
+    top[512:2304, :] = side[...].astype(F32)
+    top[2304:, :] = side_other[...].astype(F32)
     for leaf in range(4):
 
         @pl.loop(0, 1024 // 16)
@@ -160,10 +178,14 @@
     z, c, x, y = s // 2, s % 2, r // 4, r % 4
     place = jnp.stack([z, c, x, y]).astype(jnp.int32)
     own_core = ((leaf_rows // 256) % 2) == c
-    slots = (jnp.where(own_core, 0, 2048) + (leaf_rows // 512) * 256 + leaf_rows % 256).reshape(-1)
+    chips, within = leaf_rows // 512, leaf_rows % 256
+    slots = (jnp.where(own_core, 0, 2048) + chips * 256 + within).reshape(-1)
+    picks = (gathered_slot(chips, own_core, z, c) + within).reshape(-1)
 
     factors = jnp.concatenate([leaf_inv, leaf_panel], axis=1)
-    pieces, left, right = gather_factors(factors[:2], factors[2:], top_inv)
+    right = lax.all_gather(top_inv, "snode", axis=0, tiled=True, axis_index_groups=Z_GROUPS)
+    pieces, across = gather_factors(factors[:2], factors[2:], top_inv)
+    left = lax.all_gather(across, "rhs", axis=0, tiled=True)
     right_other = swap_core(right)
     inv, panel, forward, update = pl.pallas_call(
         forward_kernel,
@@ -197,28 +219,28 @@
     chip = (update[0].astype(F32) + swap_core(update[1]).astype(F32)).astype(BF)
     total = jnp.sum(exchange_z(chip).astype(F32), axis=0)
     reduced = (top_loads.astype(F32) - total).astype(BF)
-    reduced_mine, reduced_other = gather_z(reduced)
+    reduced_pieces = gather_z(reduced)
     top_solution = pl.pallas_call(
         top_kernel,
         out_shape=jax.ShapeDtypeStruct((256, 256), F32),
-        in_specs=[SMEM] + [VMEM] * 3,
+        in_specs=[SMEM] + [VMEM] * 4,
         out_specs=VMEM,
         scratch_shapes=[pltpu.VMEM((256, 4096), BF), pltpu.VMEM((4096, 256), BF)],
         compiler_params=PARAMS,
         cost_estimate=pl.CostEstimate(flops=10**9, bytes_accessed=6 * 2**20, transcendentals=0),
         name="top_solve",
-    )(place, reduced_mine, reduced_other, square_rows)
-    top_mine, top_other = gather_z(top_solution.astype(BF))
+    )(place, *reduced_pieces, square_rows)
+    top_pieces = gather_z(top_solution.astype(BF))
     leaf_solution = pl.pallas_call(
         backward_kernel,
         out_shape=jax.ShapeDtypeStruct((4, 512, 256), F32),
-        in_specs=[SMEM] + [VMEM] * 5,
+        in_specs=[SMEM] + [VMEM] * 6,
         out_specs=VMEM,
         scratch_shapes=[pltpu.VMEM((4096, 256), F32), pltpu.VMEM((1024, 256), BF)],
         compiler_params=PARAMS,
         cost_estimate=pl.CostEstimate(flops=10**10, bytes_accessed=12 * 2**20, transcendentals=0),
         name="leaf_backward",
-    )(slots, inv, panel, forward, top_mine, top_other)
+    )(picks, inv, panel, forward, *top_pieces)
     return leaf_solution, top_solution
 
 

time: 251 us -> 222 us (0.88)
  blocking collectives: 63 us -> 0 us
  waiting for transfers between devices: 53.5 us -> 88.9 us
    all_to_all x2 -> x0, blocking collectives: 63 us -> none  [exchange_z(): return lax.all_to_all(a, 'snode', 0, 0, axis_index_groups=groups)]
    ppermute x16, waiting for transfers between devices: 0.04 us -> 27.6 us  [move_rhs(): return lax.ppermute(a, 'rhs', pairs)]
    ppermute x8, waiting for transfers between devices: 18.4 us -> 24.5 us  [onward(): return lax.ppermute(b, 'snode', pairs)]
    unnamed x26 -> x29, local copies, waits for them, and re-layouts: 6.23 us -> 1.95 us
    ppermute x8, starting transfers between devices: 14 us -> 10.7 us  [onward(): return lax.ppermute(b, 'snode', pairs)]
    all_to_all x1, waiting for transfers between devices: 22.9 us -> 26 us  [exchange_z(): return lax.all_to_all(a, 'snode', 0, 0, axis_index_groups=Z_GROUPS)]
    slice x10 -> x8, local copies, waits for them, and re-layouts: 2.15 us -> 5.17 us  [far(): return (move(before[:half], 1), move(after[half:], -1))]
    ppermute x1, waiting for transfers between devices: 2.99 us -> 0.01 us  [gather_factors(): lax.ppermute(top_inv, ('snode', 'rhs'), [(16 * a + b, 16 * b + a) for a i...]
  transfers between devices with their start and end apart: 32 -> 35, of which waited for: 11 -> 17; matrix products, arithmetic and copies ran while one was open for 5% -> 7% of each run, Pallas kernels for 7% -> 8%
where the time goes in v1:
time: 222 us; the launch traced here: 221 us
  waiting for transfers between devices  88.9 us (40%)
  starting transfers between devices  62.7 us (28%)
  Pallas kernels  39.2 us (18%)
  between operations  14.1 us (6%)
  local copies, waits for them, and re-layouts  10.9 us (5%)
  other arithmetic  5.54 us (2%)
    ppermute x16, starting transfers between devices, move_rhs(): return lax.ppermute(a, 'rhs', pairs)  29.7 us
    ppermute x16, waiting for transfers between devices, move_rhs(): return lax.ppermute(a, 'rhs', pairs)  27.6 us
    all_to_all x1, waiting for transfers between devices, exchange_z(): return lax.all_to_all(a, 'snode', 0, 0, axis_index_groups=Z_GROUPS)  26 us
    ppermute x8, waiting for transfers between devices, onward(): return lax.ppermute(b, 'snode', pairs)  24.5 us
    pallas_call x1, Pallas kernels, per_device(): pl.pallas_call(backward_kernel, out_shape=jax.ShapeDtypeStruct((4, 512, 2...  17.6 us
    pallas_call x1, Pallas kernels, per_device(): pl.pallas_call(forward_kernel, out_shape=(jax.ShapeDtypeStruct((4, 512, 5...  15.3 us
    ppermute x8, starting transfers between devices, onward(): return lax.ppermute(b, 'snode', pairs)  10.7 us
    ppermute x6, starting transfers between devices, swap_core(): return lax.ppermute(a, 'snode', [(i, i ^ 1) for i in range(16)])  10.4 us
  transfers between devices with their start and end apart: 35, of which 17 were waited for; matrix products, arithmetic and copies ran while one was open for 7% of the time, Pallas kernels for 8%

profile of v1, /device:TPU:1, one launch (start us, length us, event | category | flops | bytes accessed | tf_op | source)
XLA Modules:
  0.0 221.3 jit_solution(6382848695956198335)
XLA Ops:
  7.2 0.7 all-gather.6.cloned.1.call-update
  8.0 0.9 constant_dynamic-update-slice_fusion.1
  8.9 1.0 constant_dynamic-update-slice_fusion
  9.8 0.1 fusion.11
  9.9 2.1 collective-permute-start.4
  12.0 1.4 collective-permute-start.5
  13.4 1.4 collective-permute-start
  14.8 1.4 collective-permute-start.1
  16.2 3.8 %collective-permute-start.8 = (bf16[256,256]{1,0:T(8,128)(2,1)S(1)}, bf16[256,256]{1,0:T(8,128)(2,1)S(1)}, u32[]{:S(2)}, u32[]{:S(2)}) collective-permute-start(bf16[256,256]{1,0:T(8,128)(2,1)S(1)} %copy-done.2), channel_id=1, source_target_pairs={{0,0},{1,16},{2,32},{3,48},{4,64},{5,80},{6,96},{7,112},{8,128},{9... | collective-permute-start | bytes 393224 | tf_op jit(solution)/shard_map/ppermute | solution.py:46
  20.0 3.8 %collective-permute-start.6 = (bf16[1,96,512]{2,1,0:T(8,128)(2,1)S(1)}, bf16[1,96,512]{2,1,0:T(8,128)(2,1)S(1)}, u32[]{:S(2)}, u32[]{:S(2)}) collective-permute-start(bf16[1,96,512]{2,1,0:T(8,128)(2,1)S(1)} %slice.62), channel_id=1, source_target_pairs={{0,4},{1,5},{2,6},{3,7},{4,8},{5,9},{6,10},{7,11},{8,12},{9,13},{1... | collective-permute-start | bytes 294920 | tf_op jit(solution)/shard_map/ppermute | solution.py:21
  23.9 4.3 %collective-permute-start.7 = (bf16[1,96,512]{2,1,0:T(8,128)(2,1)S(1)}, bf16[1,96,512]{2,1,0:T(8,128)(2,1)S(1)}, u32[]{:S(2)}, u32[]{:S(2)}) collective-permute-start(bf16[1,96,512]{2,1,0:T(8,128)(2,1)S(1)} %slice.63), channel_id=1, source_target_pairs={{0,12},{1,13},{2,14},{3,15},{4,0},{5,1},{6,2},{7,3},{8,4},{9,5},{1... | collective-permute-start | bytes 294920 | tf_op jit(solution)/shard_map/ppermute | solution.py:21
  28.2 0.1 collective-permute-start.2
  28.3 2.7 %collective-permute-start.3 = (bf16[1,96,512]{2,1,0:T(8,128)(2,1)S(1)}, bf16[1,96,512]{2,1,0:T(8,128)(2,1)S(1)}, u32[]{:S(2)}, u32[]{:S(2)}) collective-permute-start(bf16[1,96,512]{2,1,0:T(8,128)(2,1)S(1)} %slice.60), channel_id=1, source_target_pairs={{0,3},{1,0},{2,1},{3,2},{4,7},{5,4},{6,5},{7,6},{8,11},{9,8},{10,9... | collective-permute-start | bytes 294920 | tf_op jit(solution)/shard_map/ppermute | solution.py:21
  31.2 3.9 %collective-permute-done.6 = bf16[1,96,512]{2,1,0:T(8,128)(2,1)S(1)} collective-permute-done((bf16[1,96,512]{2,1,0:T(8,128)(2,1)S(1)}, bf16[1,96,512]{2,1,0:T(8,128)(2,1)S(1)}, u32[]{:S(2)}, u32[]{:S(2)}) %collective-permute-start.6) | collective-permute-done | bytes 98336 | tf_op jit(solution)/shard_map/ppermute | solution.py:21
  35.1 0.8 copy-done.6
  35.9 2.5 %collective-permute-start.9 = (bf16[8,96,512]{2,1,0:T(8,128)(2,1)S(1)}, bf16[8,96,512]{2,1,0:T(8,128)(2,1)S(1)}, u32[]{:S(2)}, u32[]{:S(2)}) collective-permute-start(bf16[8,96,512]{2,1,0:T(8,128)(2,1)S(1)} %constant_dynamic-update-slice_fusion.2.refs_0_), channel_id=1, source_target_pairs={{0,4},{1,5},{2,6},{3,7},{4,8},{5,9},{6,10},{7,11},{8,12},{9,13},{1... | collective-permute-start | bytes 2359304 | tf_op jit(solution)/shard_map/ppermute | solution.py:21
  38.4 1.9 collective-permute-start.10
  40.4 2.7 %collective-permute-start.14 = (bf16[8,96,512]{2,1,0:T(8,128)(2,1)}, bf16[8,96,512]{2,1,0:T(8,128)(2,1)}, u32[]{:S(2)}, u32[]{:S(2)}) collective-permute-start(bf16[8,96,512]{2,1,0:T(8,128)(2,1)} %copy-done.6), channel_id=1, source_target_pairs={{0,3},{1,0},{2,1},{3,2},{4,7},{5,4},{6,5},{7,6},{8,11},{9,8},{10,9... | collective-permute-start | bytes 2359304 | tf_op jit(solution)/shard_map/ppermute | solution.py:21
  43.1 15.4 %collective-permute-done.9.refs_1_ = bf16[8,96,512]{2,1,0:T(8,128)(2,1)S(1)} collective-permute-done((bf16[8,96,512]{2,1,0:T(8,128)(2,1)S(1)}, bf16[8,96,512]{2,1,0:T(8,128)(2,1)S(1)}, u32[]{:S(2)}, u32[]{:S(2)}) %collective-permute-start.9) | collective-permute-done | bytes 786464 | tf_op jit(solution)/shard_map/ppermute | solution.py:21
  58.4 0.8 slice.64
  59.2 0.8 slice.65
  60.0 2.7 %collective-permute-start.12 = (bf16[4,96,512]{2,1,0:T(8,128)(2,1)}, bf16[4,96,512]{2,1,0:T(8,128)(2,1)S(1)}, u32[]{:S(2)}, u32[]{:S(2)}) collective-permute-start(bf16[4,96,512]{2,1,0:T(8,128)(2,1)} %slice.65), channel_id=1, source_target_pairs={{0,12},{1,13},{2,14},{3,15},{4,0},{5,1},{6,2},{7,3},{8,4},{9,5},{1... | collective-permute-start | bytes 1179656 | tf_op jit(solution)/shard_map/ppermute | solution.py:21
  62.7 1.8 slice.66
  64.5 1.8 slice.67
  66.3 2.7 %collective-permute-start.16 = (bf16[4,96,512]{2,1,0:T(8,128)(2,1)}, bf16[4,96,512]{2,1,0:T(8,128)(2,1)}, u32[]{:S(2)}, u32[]{:S(2)}) collective-permute-start(bf16[4,96,512]{2,1,0:T(8,128)(2,1)} %slice.67), channel_id=1, source_target_pairs={{0,3},{1,0},{2,1},{3,2},{4,7},{5,4},{6,5},{7,6},{8,11},{9,8},{10,9... | collective-permute-start | bytes 1179656 | tf_op jit(solution)/shard_map/ppermute | solution.py:21
  69.0 0.1 add_bitcast_fusion
  69.1 0.1 pad_add_fusion.place
  69.1 2.2 collective-permute-done.11.refs_3_
  71.3 4.6 %collective-permute-done.15.refs_8_ = bf16[4,96,512]{2,1,0:T(8,128)(2,1)} collective-permute-done((bf16[4,96,512]{2,1,0:T(8,128)(2,1)}, bf16[4,96,512]{2,1,0:T(8,128)(2,1)}, u32[]{:S(2)}, u32[]{:S(2)}) %collective-permute-start.15) | collective-permute-done | bytes 393248 | tf_op jit(solution)/shard_map/ppermute | solution.py:21
  75.9 1.5 collective-permute-done.16.refs_9_
  77.5 15.3 %leaf_forward.1 = (bf16[4,512,512]{2,1,0:T(8,128)(2,1)}, bf16[4,1024,512]{2,1,0:T(8,128)(2,1)}, bf16[4,512,256]{2,1,0:T(8,128)(2,1)}, bf16[4096,256]{1,0:T(8,128)(2,1)}) custom-call(s32[4]{0:T(128)S(1)} %pad_add_fusion.place, s32[8,4096]{1,0:T(8,128)S(1)} %broadcast_in_dim.24.rows, bf16[4,512,256]{2,1,0:T(8,128)(2,1)} %loads.1, ...), custom_call_target="tpu_custom_call" | custom-call | flops 10000000000 | bytes 20971520 | tf_op jit(solution)/shard_map/leaf_forward/pallas_call | solution.py:190
  92.8 2.6 %fusion.10 = (bf16[2048,256]{1,0:T(8,128)(2,1)S(1)}, bf16[2048,256]{1,0:T(8,128)(2,1)}) fusion(bf16[4096,256]{1,0:T(8,128)(2,1)} %get-tuple-element.14), kind=kLoop, calls=%fused_computation.56 | loop fusion | bytes 4194304 | tf_op jit(solution)/shard_map/slice | solution.py:219
  95.4 2.5 %collective-permute-start.17 = (bf16[8,256,256]{2,1,0:T(8,128)(2,1)S(1)}, bf16[8,256,256]{2,1,0:T(8,128)(2,1)}, u32[]{:S(2)}, u32[]{:S(2)}) collective-permute-start(bf16[8,256,256]{2,1,0:T(8,128)(2,1)S(1)} %bitcast.19), channel_id=1, source_target_pairs={{0,16},{16,0},{32,48},{48,32},{64,80},{80,64},{96,112},{112,96},{1... | collective-permute-start | bytes 3145736 | tf_op jit(solution)/shard_map/ppermute | solution.py:25
  98.0 3.9 %collective-permute-done.17 = bf16[8,256,256]{2,1,0:T(8,128)(2,1)} collective-permute-done((bf16[8,256,256]{2,1,0:T(8,128)(2,1)S(1)}, bf16[8,256,256]{2,1,0:T(8,128)(2,1)}, u32[]{:S(2)}, u32[]{:S(2)}) %collective-permute-start.17) | collective-permute-done | bytes 1048608 | tf_op jit(solution)/shard_map/ppermute | solution.py:25
  101.8 2.9 %fusion = bf16[8,256,256]{2,1,0:T(8,128)(2,1)} fusion(bf16[8,256,256]{2,1,0:T(8,128)(2,1)} %bitcast.18, bf16[8,256,256]{2,1,0:T(8,128)(2,1)} %collective-permute-done.17), kind=kLoop, calls=%fused_computation.1 | loop fusion | flops 2097152 | bytes 3145728 | tf_op jit(solution)/shard_map/convert_element_type | solution.py:219
  104.7 8.0 %all-to-all-start = ((bf16[8,256,256]{2,1,0:T(8,128)(2,1)}), bf16[8,256,256]{2,1,0:T(8,128)(2,1)}, u32[]{:S(2)}, u32[]{:S(2)}) async-start(bf16[8,256,256]{2,1,0:T(8,128)(2,1)} %fusion), calls=%async_computation | async-start | bytes 2097152 | tf_op jit(solution)/shard_map/all_to_all | solution.py:56
  112.8 3.2 %top_square.1 = bf16[256,256]{1,0:T(8,128)(2,1)} custom-call(s32[4]{0:T(128)S(1)} %pad_add_fusion.place, bf16[4,512,256]{2,1,0:T(8,128)(2,1)S(1)} %copy-done.1, bf16[4096,256]{1,0:T(8,128)(2,1)} %all-gather.4.cloned.1.call-done.left, bf16[2048,256]{1,0:T(8,128)(2,1)S(1)} %copy-done, bf16[2048,256]{1,0:T(8,128)(2,1)S(1)} %collective-permute-done.24.right_other), custom_call_target="tpu_custom_call" | custom-call | flops 1000000000 | bytes 6291456 | tf_op jit(solution)/shard_map/top_square/pallas_call | solution.py:206
  116.0 26.0 %all-to-all-done = bf16[8,256,256]{2,1,0:T(8,128)(2,1)} async-done(((bf16[8,256,256]{2,1,0:T(8,128)(2,1)}), bf16[8,256,256]{2,1,0:T(8,128)(2,1)}, u32[]{:S(2)}, u32[]{:S(2)}) %all-to-all-start) | async-done | bytes 1048608 | tf_op jit(solution)/shard_map/all_to_all | solution.py:56
  142.1 1.4 convert_reduce_fusion
  143.5 0.6 collective-permute-start.18
  144.1 1.0 collective-permute-done.18
  145.1 0.2 collective-permute-start.20
  145.3 0.4 collective-permute-start.19
  145.7 8.5 %collective-permute-done.20 = bf16[512,256]{1,0:T(8,128)(2,1)S(1)} collective-permute-done((bf16[512,256]{1,0:T(8,128)(2,1)S(1)}, bf16[512,256]{1,0:T(8,128)(2,1)S(1)}, u32[]{:S(2)}, u32[]{:S(2)}) %collective-permute-start.20) | collective-permute-done | bytes 262176 | tf_op jit(solution)/shard_map/ppermute | solution.py:62
  154.2 1.3 collective-permute-start.22
  155.5 4.3 %collective-permute-done.21 = bf16[512,256]{1,0:T(8,128)(2,1)S(1)} collective-permute-done((bf16[512,256]{1,0:T(8,128)(2,1)S(1)}, bf16[512,256]{1,0:T(8,128)(2,1)S(1)}, u32[]{:S(2)}, u32[]{:S(2)}) %collective-permute-start.21) | collective-permute-done | bytes 262176 | tf_op jit(solution)/shard_map/ppermute | solution.py:62
  159.8 2.0 collective-permute-done.22
  161.8 3.0 %collective-permute-start.23 = (bf16[1792,256]{1,0:T(8,128)(2,1)S(1)}, bf16[1792,256]{1,0:T(8,128)(2,1)S(1)}, u32[]{:S(2)}, u32[]{:S(2)}) collective-permute-start(bf16[1792,256]{1,0:T(8,128)(2,1)S(1)} %constant_dynamic-update-slice_fusion.12.side), channel_id=1, source_target_pairs={{0,16},{16,0},{32,48},{48,32},{64,80},{80,64},{96,112},{112,96},{1... | collective-permute-start | bytes 2752520 | tf_op jit(solution)/shard_map/ppermute | solution.py:25
  164.8 2.1 collective-permute-done.23.side_other
  166.9 3.1 %top_solve.1 = f32[256,256]{1,0:T(8,128)} custom-call(s32[4]{0:T(128)S(1)} %pad_add_fusion.place, bf16[512,256]{1,0:T(8,128)(2,1)S(1)} %pad_maximum_fusion.own_chip, bf16[1792,256]{1,0:T(8,128)(2,1)S(1)} %constant_dynamic-update-slice_fusion.12.side, bf16[1792,256]{1,0:T(8,128)(2,1)S(1)} %collective-permute-done.23.side_other, ...), custom_call_target="tpu_custom_call" | custom-call | flops 1000000000 | bytes 6291456 | tf_op jit(solution)/shard_map/top_solve/pallas_call | solution.py:223
  170.1 1.0 convert_element_type.31
  171.0 0.7 collective-permute-start.25
  171.7 1.0 collective-permute-done.25
  172.7 3.6 %collective-permute-start.27 = (bf16[512,256]{1,0:T(8,128)(2,1)S(1)}, bf16[512,256]{1,0:T(8,128)(2,1)S(1)}, u32[]{:S(2)}, u32[]{:S(2)}) collective-permute-start(bf16[512,256]{1,0:T(8,128)(2,1)S(1)} %pad_maximum_fusion.1.own_chip), channel_id=1, source_target_pairs={{0,64},{16,208},{32,96},{48,240},{64,128},{80,16},{96,160},{112,48... | collective-permute-start | bytes 786440 | tf_op jit(solution)/shard_map/ppermute | solution.py:62
  176.3 1.1 collective-permute-start.26
  177.4 5.0 %collective-permute-done.27 = bf16[512,256]{1,0:T(8,128)(2,1)S(1)} collective-permute-done((bf16[512,256]{1,0:T(8,128)(2,1)S(1)}, bf16[512,256]{1,0:T(8,128)(2,1)S(1)}, u32[]{:S(2)}, u32[]{:S(2)}) %collective-permute-start.27) | collective-permute-done | bytes 262176 | tf_op jit(solution)/shard_map/ppermute | solution.py:62
  182.4 2.3 %collective-permute-start.28 = (bf16[512,256]{1,0:T(8,128)(2,1)S(1)}, bf16[512,256]{1,0:T(8,128)(2,1)S(1)}, u32[]{:S(2)}, u32[]{:S(2)}) collective-permute-start(bf16[512,256]{1,0:T(8,128)(2,1)S(1)} %collective-permute-done.27), channel_id=1, source_target_pairs={{0,32},{16,240},{32,64},{48,16},{64,96},{80,48},{96,128},{112,80},... | collective-permute-start | bytes 786440 | tf_op jit(solution)/shard_map/ppermute | solution.py:62
  184.7 1.9 collective-permute-start.29
  186.6 1.5 collective-permute-done.28
  188.2 3.3 %collective-permute-done.29 = bf16[256,256]{1,0:T(8,128)(2,1)S(1)} collective-permute-done((bf16[256,256]{1,0:T(8,128)(2,1)S(1)}, bf16[256,256]{1,0:T(8,128)(2,1)S(1)}, u32[]{:S(2)}, u32[]{:S(2)}) %collective-permute-start.29) | collective-permute-done | bytes 131104 | tf_op jit(solution)/shard_map/ppermute | solution.py:62
  191.4 3.6 %collective-permute-start.30 = (bf16[1792,256]{1,0:T(8,128)(2,1)S(1)}, bf16[1792,256]{1,0:T(8,128)(2,1)S(1)}, u32[]{:S(2)}, u32[]{:S(2)}) collective-permute-start(bf16[1792,256]{1,0:T(8,128)(2,1)S(1)} %constant_dynamic-update-slice_fusion.16.side), channel_id=1, source_target_pairs={{0,16},{16,0},{32,48},{48,32},{64,80},{80,64},{96,112},{112,96},{1... | collective-permute-start | bytes 2752520 | tf_op jit(solution)/shard_map/ppermute | solution.py:25
  195.0 0.1 fusion.4
  195.1 2.0 collective-permute-done.30.side_other
  197.1 17.6 %leaf_backward.1 = f32[4,512,256]{2,1,0:T(8,128)} custom-call(s32[4096]{0:T(1024)S(1)} %bitcast.17, bf16[4,512,512]{2,1,0:T(8,128)(2,1)} %get-tuple-element.11.inv, bf16[4,1024,512]{2,1,0:T(8,128)(2,1)} %get-tuple-element.12.panel, bf16[4,512,256]{2,1,0:T(8,128)(2,1)S(1)} %copy-done.1, bf16[512,256]{1,0:T(8,128)(2,1)S(1)} %pad_maximum_fusion.1.own_chip, ...), custom_call_target="tpu_custom_call" | custom-call | flops 10000000000 | bytes 12582912 | tf_op jit(solution)/shard_map/leaf_backward/pallas_call | solution.py:234
  (69 shorter events, 0.6 us)
Async XLA Ops:
  7.2 9.1 %copy-start.2 = (bf16[256,256]{1,0:T(8,128)(2,1)S(1)}, bf16[256,256]{1,0:T(8,128)(2,1)}, u32[]{:S(2)}) copy-start(bf16[256,256]{1,0:T(8,128)(2,1)} %param.10) | copy-start | bytes 393220
  7.2 90.8 %all-gather.6.cloned.1.call-start = ((), (), s32[]{:S(2)}) async-start(), calls=%async_computation.2 | async-start | bytes 1179648 | tf_op jit(solution)/shard_map/all_gather | solution.py:186
  7.9 104.9 %all-gather.4.cloned.1.call-start = ((), (), s32[]{:S(2)}) async-start(), calls=%async_computation.1 | async-start | bytes 2228224 | tf_op jit(solution)/shard_map/all_gather | solution.py:188
  9.9 10.1 %collective-permute-start.4 = (bf16[2,96,512]{2,1,0:T(8,128)(2,1)S(1)}, bf16[2,96,512]{2,1,0:T(8,128)(2,1)S(1)}, u32[]{:S(2)}, u32[]{:S(2)}) collective-permute-start(bf16[2,96,512]{2,1,0:T(8,128)(2,1)S(1)} %get-tuple-element.20), channel_id=1, source_target_pairs={{0,4},{1,5},{2,6},{3,7},{4,8},{5,9},{6,10},{7,11},{8,12},{9,13},{1... | collective-permute-start | bytes 589832 | tf_op jit(solution)/shard_map/ppermute | solution.py:21
  12.0 11.8 %collective-permute-start.5 = (bf16[2,96,512]{2,1,0:T(8,128)(2,1)S(1)}, bf16[2,96,512]{2,1,0:T(8,128)(2,1)S(1)}, u32[]{:S(2)}, u32[]{:S(2)}) collective-permute-start(bf16[2,96,512]{2,1,0:T(8,128)(2,1)S(1)} %get-tuple-element.20), channel_id=1, source_target_pairs={{0,12},{1,13},{2,14},{3,15},{4,0},{5,1},{6,2},{7,3},{8,4},{9,5},{1... | collective-permute-start | bytes 589832 | tf_op jit(solution)/shard_map/ppermute | solution.py:21
  13.4 14.8 %collective-permute-start = (bf16[2,96,512]{2,1,0:T(8,128)(2,1)S(1)}, bf16[2,96,512]{2,1,0:T(8,128)(2,1)S(1)}, u32[]{:S(2)}, u32[]{:S(2)}) collective-permute-start(bf16[2,96,512]{2,1,0:T(8,128)(2,1)S(1)} %get-tuple-element.23), channel_id=1, source_target_pairs={{0,1},{1,2},{2,3},{3,0},{4,5},{5,6},{6,7},{7,4},{8,9},{9,10},{10,1... | collective-permute-start | bytes 589832 | tf_op jit(solution)/shard_map/ppermute | solution.py:21
  14.8 13.5 %collective-permute-start.1 = (bf16[2,96,512]{2,1,0:T(8,128)(2,1)S(1)}, bf16[2,96,512]{2,1,0:T(8,128)(2,1)S(1)}, u32[]{:S(2)}, u32[]{:S(2)}) collective-permute-start(bf16[2,96,512]{2,1,0:T(8,128)(2,1)S(1)} %get-tuple-element.23), channel_id=1, source_target_pairs={{0,3},{1,0},{2,1},{3,2},{4,7},{5,4},{6,5},{7,6},{8,11},{9,8},{10,9... | collective-permute-start | bytes 589832 | tf_op jit(solution)/shard_map/ppermute | solution.py:21
  16.2 19.7 %collective-permute-start.8 = (bf16[256,256]{1,0:T(8,128)(2,1)S(1)}, bf16[256,256]{1,0:T(8,128)(2,1)S(1)}, u32[]{:S(2)}, u32[]{:S(2)}) collective-permute-start(bf16[256,256]{1,0:T(8,128)(2,1)S(1)} %copy-done.2), channel_id=1, source_target_pairs={{0,0},{1,16},{2,32},{3,48},{4,64},{5,80},{6,96},{7,112},{8,128},{9... | collective-permute-start | bytes 393224 | tf_op jit(solution)/shard_map/ppermute | solution.py:46
  20.0 15.0 %collective-permute-start.6 = (bf16[1,96,512]{2,1,0:T(8,128)(2,1)S(1)}, bf16[1,96,512]{2,1,0:T(8,128)(2,1)S(1)}, u32[]{:S(2)}, u32[]{:S(2)}) collective-permute-start(bf16[1,96,512]{2,1,0:T(8,128)(2,1)S(1)} %slice.62), channel_id=1, source_target_pairs={{0,4},{1,5},{2,6},{3,7},{4,8},{5,9},{6,10},{7,11},{8,12},{9,13},{1... | collective-permute-start | bytes 294920 | tf_op jit(solution)/shard_map/ppermute | solution.py:21
  23.9 11.2 %collective-permute-start.7 = (bf16[1,96,512]{2,1,0:T(8,128)(2,1)S(1)}, bf16[1,96,512]{2,1,0:T(8,128)(2,1)S(1)}, u32[]{:S(2)}, u32[]{:S(2)}) collective-permute-start(bf16[1,96,512]{2,1,0:T(8,128)(2,1)S(1)} %slice.63), channel_id=1, source_target_pairs={{0,12},{1,13},{2,14},{3,15},{4,0},{5,1},{6,2},{7,3},{8,4},{9,5},{1... | collective-permute-start | bytes 294920 | tf_op jit(solution)/shard_map/ppermute | solution.py:21
  28.2 6.9 %collective-permute-start.2 = (bf16[1,96,512]{2,1,0:T(8,128)(2,1)S(1)}, bf16[1,96,512]{2,1,0:T(8,128)(2,1)S(1)}, u32[]{:S(2)}, u32[]{:S(2)}) collective-permute-start(bf16[1,96,512]{2,1,0:T(8,128)(2,1)S(1)} %slice.59), channel_id=1, source_target_pairs={{0,1},{1,2},{2,3},{3,0},{4,5},{5,6},{6,7},{7,4},{8,9},{9,10},{10,1... | collective-permute-start | bytes 294920 | tf_op jit(solution)/shard_map/ppermute | solution.py:21
  28.3 6.8 %collective-permute-start.3 = (bf16[1,96,512]{2,1,0:T(8,128)(2,1)S(1)}, bf16[1,96,512]{2,1,0:T(8,128)(2,1)S(1)}, u32[]{:S(2)}, u32[]{:S(2)}) collective-permute-start(bf16[1,96,512]{2,1,0:T(8,128)(2,1)S(1)} %slice.60), channel_id=1, source_target_pairs={{0,3},{1,0},{2,1},{3,2},{4,7},{5,4},{6,5},{7,6},{8,11},{9,8},{10,9... | collective-permute-start | bytes 294920 | tf_op jit(solution)/shard_map/ppermute | solution.py:21
  31.1 37.8 %copy-start.5 = (s32[4,1024]{1,0:T(4,128)S(1)}, s32[4,1024]{1,0:T(4,128)}, u32[]{:S(2)}) copy-start(s32[4,1024]{1,0:T(4,128)} %param.8) | copy-start | bytes 49156
  35.1 0.9 copy-start.6
  35.9 7.1 %copy-start.3 = (bf16[256,256]{1,0:T(8,128)(2,1)}, bf16[256,256]{1,0:T(8,128)(2,1)S(1)}, u32[]{:S(2)}) copy-start(bf16[256,256]{1,0:T(8,128)(2,1)S(1)} %collective-permute-done.8) | copy-start | bytes 393220
  35.9 22.5 %collective-permute-start.9 = (bf16[8,96,512]{2,1,0:T(8,128)(2,1)S(1)}, bf16[8,96,512]{2,1,0:T(8,128)(2,1)S(1)}, u32[]{:S(2)}, u32[]{:S(2)}) collective-permute-start(bf16[8,96,512]{2,1,0:T(8,128)(2,1)S(1)} %constant_dynamic-update-slice_fusion.2.refs_0_), channel_id=1, source_target_pairs={{0,4},{1,5},{2,6},{3,7},{4,8},{5,9},{6,10},{7,11},{8,12},{9,13},{1... | collective-permute-start | bytes 2359304 | tf_op jit(solution)/shard_map/ppermute | solution.py:21
  38.4 20.8 %collective-permute-start.10 = (bf16[8,96,512]{2,1,0:T(8,128)(2,1)S(1)}, bf16[8,96,512]{2,1,0:T(8,128)(2,1)S(1)}, u32[]{:S(2)}, u32[]{:S(2)}) collective-permute-start(bf16[8,96,512]{2,1,0:T(8,128)(2,1)S(1)} %constant_dynamic-update-slice_fusion.2.refs_0_), channel_id=1, source_target_pairs={{0,12},{1,13},{2,14},{3,15},{4,0},{5,1},{6,2},{7,3},{8,4},{9,5},{1... | collective-permute-start | bytes 2359304 | tf_op jit(solution)/shard_map/ppermute | solution.py:21
  40.4 22.3 %collective-permute-start.13 = (bf16[8,96,512]{2,1,0:T(8,128)(2,1)}, bf16[8,96,512]{2,1,0:T(8,128)(2,1)}, u32[]{:S(2)}, u32[]{:S(2)}) collective-permute-start(bf16[8,96,512]{2,1,0:T(8,128)(2,1)} %copy-done.6), channel_id=1, source_target_pairs={{0,1},{1,2},{2,3},{3,0},{4,5},{5,6},{6,7},{7,4},{8,9},{9,10},{10,1... | collective-permute-start | bytes 2359304 | tf_op jit(solution)/shard_map/ppermute | solution.py:21
  40.4 24.1 %collective-permute-start.14 = (bf16[8,96,512]{2,1,0:T(8,128)(2,1)}, bf16[8,96,512]{2,1,0:T(8,128)(2,1)}, u32[]{:S(2)}, u32[]{:S(2)}) collective-permute-start(bf16[8,96,512]{2,1,0:T(8,128)(2,1)} %copy-done.6), channel_id=1, source_target_pairs={{0,3},{1,0},{2,1},{3,2},{4,7},{5,4},{6,5},{7,6},{8,11},{9,8},{10,9... | collective-permute-start | bytes 2359304 | tf_op jit(solution)/shard_map/ppermute | solution.py:21
  59.2 12.1 %collective-permute-start.11 = (bf16[4,96,512]{2,1,0:T(8,128)(2,1)}, bf16[4,96,512]{2,1,0:T(8,128)(2,1)S(1)}, u32[]{:S(2)}, u32[]{:S(2)}) collective-permute-start(bf16[4,96,512]{2,1,0:T(8,128)(2,1)} %slice.64), channel_id=1, source_target_pairs={{0,4},{1,5},{2,6},{3,7},{4,8},{5,9},{6,10},{7,11},{8,12},{9,13},{1... | collective-permute-start | bytes 1179656 | tf_op jit(solution)/shard_map/ppermute | solution.py:21
  60.0 11.3 %collective-permute-start.12 = (bf16[4,96,512]{2,1,0:T(8,128)(2,1)}, bf16[4,96,512]{2,1,0:T(8,128)(2,1)S(1)}, u32[]{:S(2)}, u32[]{:S(2)}) collective-permute-start(bf16[4,96,512]{2,1,0:T(8,128)(2,1)} %slice.65), channel_id=1, source_target_pairs={{0,12},{1,13},{2,14},{3,15},{4,0},{5,1},{6,2},{7,3},{8,4},{9,5},{1... | collective-permute-start | bytes 1179656 | tf_op jit(solution)/shard_map/ppermute | solution.py:21
  64.5 11.4 %collective-permute-start.15 = (bf16[4,96,512]{2,1,0:T(8,128)(2,1)}, bf16[4,96,512]{2,1,0:T(8,128)(2,1)}, u32[]{:S(2)}, u32[]{:S(2)}) collective-permute-start(bf16[4,96,512]{2,1,0:T(8,128)(2,1)} %slice.66), channel_id=1, source_target_pairs={{0,1},{1,2},{2,3},{3,0},{4,5},{5,6},{6,7},{7,4},{8,9},{9,10},{10,1... | collective-permute-start | bytes 1179656 | tf_op jit(solution)/shard_map/ppermute | solution.py:21
  66.3 11.2 %collective-permute-start.16 = (bf16[4,96,512]{2,1,0:T(8,128)(2,1)}, bf16[4,96,512]{2,1,0:T(8,128)(2,1)}, u32[]{:S(2)}, u32[]{:S(2)}) collective-permute-start(bf16[4,96,512]{2,1,0:T(8,128)(2,1)} %slice.67), channel_id=1, source_target_pairs={{0,3},{1,0},{2,1},{3,2},{4,7},{5,4},{6,5},{7,6},{8,11},{9,8},{10,9... | collective-permute-start | bytes 1179656 | tf_op jit(solution)/shard_map/ppermute | solution.py:21
  95.4 6.4 %collective-permute-start.17 = (bf16[8,256,256]{2,1,0:T(8,128)(2,1)S(1)}, bf16[8,256,256]{2,1,0:T(8,128)(2,1)}, u32[]{:S(2)}, u32[]{:S(2)}) collective-permute-start(bf16[8,256,256]{2,1,0:T(8,128)(2,1)S(1)} %bitcast.19), channel_id=1, source_target_pairs={{0,16},{16,0},{32,48},{48,32},{64,80},{80,64},{96,112},{112,96},{1... | collective-permute-start | bytes 3145736 | tf_op jit(solution)/shard_map/ppermute | solution.py:25
  98.0 14.8 %collective-permute-start.24 = (bf16[2048,256]{1,0:T(8,128)(2,1)}, bf16[2048,256]{1,0:T(8,128)(2,1)S(1)}, u32[]{:S(2)}, u32[]{:S(2)}) collective-permute-start(bf16[2048,256]{1,0:T(8,128)(2,1)} %all-gather.6.cloned.1.call-done.right), channel_id=1, source_target_pairs={{0,16},{16,0},{32,48},{48,32},{64,80},{80,64},{96,112},{112,96},{1... | collective-permute-start | bytes 3145736 | tf_op jit(solution)/shard_map/ppermute | solution.py:25
  101.8 11.0 %copy-start = (bf16[2048,256]{1,0:T(8,128)(2,1)S(1)}, bf16[2048,256]{1,0:T(8,128)(2,1)}, u32[]{:S(2)}) copy-start(bf16[2048,256]{1,0:T(8,128)(2,1)} %all-gather.6.cloned.1.call-done.right) | copy-start | bytes 3145732
  101.8 11.0 %copy-start.1 = (bf16[4,512,256]{2,1,0:T(8,128)(2,1)S(1)}, bf16[4,512,256]{2,1,0:T(8,128)(2,1)}, u32[]{:S(2)}) copy-start(bf16[4,512,256]{2,1,0:T(8,128)(2,1)} %get-tuple-element.13.after.forward) | copy-start | bytes 3145732
  104.7 37.3 %all-to-all-start = ((bf16[8,256,256]{2,1,0:T(8,128)(2,1)}), bf16[8,256,256]{2,1,0:T(8,128)(2,1)}, u32[]{:S(2)}, u32[]{:S(2)}) async-start(bf16[8,256,256]{2,1,0:T(8,128)(2,1)} %fusion), calls=%async_computation | async-start | bytes 2097152 | tf_op jit(solution)/shard_map/all_to_all | solution.py:56
  112.7 54.2 %all-gather.8.cloned.1.call-start = ((), (), s32[]{:S(2)}) async-start(), calls=%async_computation.3 | async-start | bytes 2228224 | tf_op jit(solution)/shard_map/all_gather | solution.py:216
  112.8 30.6 %copy-start.4 = (bf16[256,256]{1,0:T(8,128)(2,1)S(1)}, bf16[256,256]{1,0:T(8,128)(2,1)}, u32[]{:S(2)}) copy-start(bf16[256,256]{1,0:T(8,128)(2,1)} %param.11) | copy-start | bytes 393220
  143.5 1.6 collective-permute-start.18
  145.1 9.1 %collective-permute-start.20 = (bf16[512,256]{1,0:T(8,128)(2,1)S(1)}, bf16[512,256]{1,0:T(8,128)(2,1)S(1)}, u32[]{:S(2)}, u32[]{:S(2)}) collective-permute-start(bf16[512,256]{1,0:T(8,128)(2,1)S(1)} %pad_maximum_fusion.own_chip), channel_id=1, source_target_pairs={{0,64},{16,208},{32,96},{48,240},{64,128},{80,16},{96,160},{112,48... | collective-permute-start | bytes 786440 | tf_op jit(solution)/shard_map/ppermute | solution.py:62
  145.3 10.2 %collective-permute-start.19 = (bf16[512,256]{1,0:T(8,128)(2,1)S(1)}, bf16[512,256]{1,0:T(8,128)(2,1)S(1)}, u32[]{:S(2)}, u32[]{:S(2)}) collective-permute-start(bf16[512,256]{1,0:T(8,128)(2,1)S(1)} %pad_maximum_fusion.own_chip), channel_id=1, source_target_pairs={{0,32},{16,240},{32,64},{48,16},{64,96},{80,48},{96,128},{112,80},... | collective-permute-start | bytes 786440 | tf_op jit(solution)/shard_map/ppermute | solution.py:62
  154.2 5.6 %collective-permute-start.21 = (bf16[512,256]{1,0:T(8,128)(2,1)S(1)}, bf16[512,256]{1,0:T(8,128)(2,1)S(1)}, u32[]{:S(2)}, u32[]{:S(2)}) collective-permute-start(bf16[512,256]{1,0:T(8,128)(2,1)S(1)} %collective-permute-done.20), channel_id=1, source_target_pairs={{0,32},{16,240},{32,64},{48,16},{64,96},{80,48},{96,128},{112,80},... | collective-permute-start | bytes 786440 | tf_op jit(solution)/shard_map/ppermute | solution.py:62
  154.2 7.6 %collective-permute-start.22 = (bf16[256,256]{1,0:T(8,128)(2,1)S(1)}, bf16[256,256]{1,0:T(8,128)(2,1)S(1)}, u32[]{:S(2)}, u32[]{:S(2)}) collective-permute-start(bf16[256,256]{1,0:T(8,128)(2,1)S(1)} %slice.68), channel_id=1, source_target_pairs={{0,64},{16,208},{32,96},{48,240},{64,128},{80,16},{96,160},{112,48... | collective-permute-start | bytes 393224 | tf_op jit(solution)/shard_map/ppermute | solution.py:62
  161.8 5.1 %collective-permute-start.23 = (bf16[1792,256]{1,0:T(8,128)(2,1)S(1)}, bf16[1792,256]{1,0:T(8,128)(2,1)S(1)}, u32[]{:S(2)}, u32[]{:S(2)}) collective-permute-start(bf16[1792,256]{1,0:T(8,128)(2,1)S(1)} %constant_dynamic-update-slice_fusion.12.side), channel_id=1, source_target_pairs={{0,16},{16,0},{32,48},{48,32},{64,80},{80,64},{96,112},{112,96},{1... | collective-permute-start | bytes 2752520 | tf_op jit(solution)/shard_map/ppermute | solution.py:25
  171.0 1.7 collective-permute-start.25
  172.7 9.7 %collective-permute-start.27 = (bf16[512,256]{1,0:T(8,128)(2,1)S(1)}, bf16[512,256]{1,0:T(8,128)(2,1)S(1)}, u32[]{:S(2)}, u32[]{:S(2)}) collective-permute-start(bf16[512,256]{1,0:T(8,128)(2,1)S(1)} %pad_maximum_fusion.1.own_chip), channel_id=1, source_target_pairs={{0,64},{16,208},{32,96},{48,240},{64,128},{80,16},{96,160},{112,48... | collective-permute-start | bytes 786440 | tf_op jit(solution)/shard_map/ppermute | solution.py:62
  176.3 10.3 %collective-permute-start.26 = (bf16[512,256]{1,0:T(8,128)(2,1)S(1)}, bf16[512,256]{1,0:T(8,128)(2,1)S(1)}, u32[]{:S(2)}, u32[]{:S(2)}) collective-permute-start(bf16[512,256]{1,0:T(8,128)(2,1)S(1)} %pad_maximum_fusion.1.own_chip), channel_id=1, source_target_pairs={{0,32},{16,240},{32,64},{48,16},{64,96},{80,48},{96,128},{112,80},... | collective-permute-start | bytes 786440 | tf_op jit(solution)/shard_map/ppermute | solution.py:62
  182.4 5.7 %collective-permute-start.28 = (bf16[512,256]{1,0:T(8,128)(2,1)S(1)}, bf16[512,256]{1,0:T(8,128)(2,1)S(1)}, u32[]{:S(2)}, u32[]{:S(2)}) collective-permute-start(bf16[512,256]{1,0:T(8,128)(2,1)S(1)} %collective-permute-done.27), channel_id=1, source_target_pairs={{0,32},{16,240},{32,64},{48,16},{64,96},{80,48},{96,128},{112,80},... | collective-permute-start | bytes 786440 | tf_op jit(solution)/shard_map/ppermute | solution.py:62
  184.7 6.7 %collective-permute-start.29 = (bf16[256,256]{1,0:T(8,128)(2,1)S(1)}, bf16[256,256]{1,0:T(8,128)(2,1)S(1)}, u32[]{:S(2)}, u32[]{:S(2)}) collective-permute-start(bf16[256,256]{1,0:T(8,128)(2,1)S(1)} %slice.69), channel_id=1, source_target_pairs={{0,64},{16,208},{32,96},{48,240},{64,128},{80,16},{96,160},{112,48... | collective-permute-start | bytes 393224 | tf_op jit(solution)/shard_map/ppermute | solution.py:62
  191.4 5.7 %collective-permute-start.30 = (bf16[1792,256]{1,0:T(8,128)(2,1)S(1)}, bf16[1792,256]{1,0:T(8,128)(2,1)S(1)}, u32[]{:S(2)}, u32[]{:S(2)}) collective-permute-start(bf16[1792,256]{1,0:T(8,128)(2,1)S(1)} %constant_dynamic-update-slice_fusion.16.side), channel_id=1, source_target_pairs={{0,16},{16,0},{32,48},{48,32},{64,80},{80,64},{96,112},{112,96},{1... | collective-permute-start | bytes 2752520 | tf_op jit(solution)/shard_map/ppermute | solution.py:25
Sparse Core Ops, SparseCore 0:
  9.8 43.4 all-gather.5
  56.3 51.9 all-gather.3
  116.6 48.8 all-gather.7
